TPU v7x, 32 devices: a whole 2x2x4 slice. The times are simulated.
32 devices in a mesh: groups: 2 (over y), ctx: 8 (over z, x), ch: 2 (over core).
Axes of the slice: x: 2, y: 2, z: 4, core: 2. Of those that a mesh axis runs over, the one named last changes fastest.
Arguments:
- gate_stream: bfloat16 [4096, 512], P(('groups', 'ctx'), 'ch'), parts along dimension 0, may hold values from -6 to 6
- outer_stream: bfloat16 [4096, 512], P(('groups', 'ctx'), 'ch'), parts along dimension 0, may hold values from -6 to 6
- value_stream: bfloat16 [4096, 512], P(('groups', 'ctx'), 'ch'), parts along dimension 0, may hold values from -6 to 6
- short_weight: bfloat16 [3, 3, 512], P(None, None, 'ch'), may hold values from -3.5 to 3.5
- long_filter: bfloat16 [2048, 512], P('ctx', 'ch'), may hold values from -0.125 to 0.125
- skip_gain: float32 [512], P('ch'), may hold values from -4 to 4
Outputs:
- output_rows: bfloat16 [4096, 512], P(('groups', 'ctx'), 'ch'), parts along dimension 0
There are 2 independent parts, one for each index of `groups`. A program takes and returns all parts, laid end to end along the dimension named above; an argument that names none is the same for every part. Nothing has to cross between parts.
All inputs are finite; a program needn't handle non-finite values.
Results may differ from a plain program's by a relative error of at most 0.001.
Values may be sent and summed in bfloat16 or wider, within the bound.
A program may use at most 64 MiB of HBM per device.

v0:
```python
import math

import jax
import jax.numpy as jnp
from jax import lax
from jax.sharding import PartitionSpec as P

full_precision = lax.Precision.HIGHEST


def passed_along(block, axis, distance):
    devices = range(lax.axis_size(axis))
    route = [(i - distance, i) for i in devices if i - distance in devices]
    return lax.ppermute(block, axis, route)


def from_partner(value, axis, apart):
    mask = 2**apart
    pairs = [(source, source ^ mask) for source in range(lax.axis_size(axis))]
    return lax.ppermute(value, axis, pairs)


def phase_table(first_ids, second, period):
    product = jnp.outer(first_ids, second) % period
    return product.astype(jnp.float32) * (2.0 * math.pi / period)


def rotate(real_part, imag_part, cosine, sine_part):
    return (real_part * cosine - imag_part * sine_part, real_part * sine_part + imag_part * cosine)


def causal_short(stream, rim_rows, kernel):
    taps_count = kernel.shape[0]
    extended = jnp.concatenate([rim_rows, stream], axis=0).astype(jnp.float32)
    length = stream.shape[0]
    summed = jnp.zeros((length, stream.shape[1]), jnp.float32)
    for offset in range(taps_count):
        begin_at = taps_count - 1 - offset
        summed = (
            summed + kernel[offset].astype(jnp.float32) * extended[begin_at : begin_at + length]
        )
    return summed


def along_rows(real_part, imag_part, direction):
    row_count = real_part.shape[-2]
    row_ids = jnp.arange(row_count, dtype=jnp.int32)
    phases = phase_table(row_ids, row_ids, row_count)
    cosine = jnp.cos(phases)
    sine_part = jnp.sin(phases) * direction
    out_real = jnp.einsum(
        "kj,...jc->...kc", cosine, real_part, precision=full_precision
    ) - jnp.einsum("kj,...jc->...kc", sine_part, imag_part, precision=full_precision)
    out_imag = jnp.einsum(
        "kj,...jc->...kc", cosine, imag_part, precision=full_precision
    ) + jnp.einsum("kj,...jc->...kc", sine_part, real_part, precision=full_precision)
    return (out_real, out_imag)


def body(gate_stream, outer_stream, value_stream, short_weight, long_filter, skip_gain):
    rows_local = gate_stream.shape[0]
    rim_count = short_weight.shape[1] - 1
    tail_rows = jnp.stack(
        [
            gate_stream[rows_local - rim_count :],
            outer_stream[rows_local - rim_count :],
            value_stream[rows_local - rim_count :],
        ]
    )
    rim_block = passed_along(tail_rows, "ctx", 1)
    gate_conv = causal_short(gate_stream, rim_block[0], short_weight[0])
    outer_conv = causal_short(outer_stream, rim_block[1], short_weight[1])
    value_conv = causal_short(value_stream, rim_block[2], short_weight[2])
    gated_value = gate_conv * value_conv
    signals = jnp.stack([gated_value, long_filter.astype(jnp.float32)])
    parts_count = lax.axis_size("ctx")
    device = lax.axis_index("ctx")
    seq_total = rows_local * parts_count
    local_rows = jnp.arange(rows_local, dtype=jnp.int32)
    sections = parts_count.bit_length() - 1
    slot_ids = jnp.arange(2, dtype=jnp.int32)
    slot_phase = -math.pi * (device * slot_ids).astype(jnp.float32) / parts_count
    cos_slot = jnp.cos(slot_phase)[None, :, None, None]
    sin_slot = jnp.sin(slot_phase)[None, :, None, None]
    expanded = signals[:, None]
    current = jnp.stack([expanded * cos_slot, expanded * sin_slot])
    for bit_index in reversed(range(sections)):
        half_span = 1 << bit_index
        received = from_partner(current, "ctx", bit_index)
        is_lower = jnp.bitwise_and(device, half_span) == 0
        offset_phase = (
            -math.pi * jnp.bitwise_and(device, half_span - 1).astype(jnp.float32) / half_span
        )
        differ = received - current
        turned = jnp.stack(
            rotate(differ[0], differ[1], jnp.cos(offset_phase), jnp.sin(offset_phase))
        )
        current = jnp.where(is_lower, current + received, turned)
    reversed_index = jnp.zeros((), jnp.int32)
    for bit_index in range(sections):
        reversed_index = reversed_index + jnp.left_shift(
            jnp.bitwise_and(jnp.right_shift(device, bit_index), 1), sections - 1 - bit_index
        )
    freq_first = 2 * reversed_index + slot_ids
    twist_phase = phase_table(local_rows, freq_first, 2 * seq_total).T
    twist_cos = jnp.cos(twist_phase)[:, :, None]
    twist_sin = jnp.sin(twist_phase)[:, :, None]
    real_part, imag_part = rotate(current[0], current[1], twist_cos, -twist_sin)
    spec_real, spec_imag = along_rows(real_part, imag_part, -1.0)
    prod_real = spec_real[0] * spec_real[1] - spec_imag[0] * spec_imag[1]
    prod_imag = spec_real[0] * spec_imag[1] + spec_imag[0] * spec_real[1]
    back_real, back_imag = along_rows(prod_real, prod_imag, 1.0)
    current = jnp.stack(rotate(back_real, back_imag, twist_cos, twist_sin))
    for bit_index in range(sections):
        half_span = 1 << bit_index
        received = from_partner(current, "ctx", bit_index)
        is_lower = jnp.bitwise_and(device, half_span) == 0
        offset_phase = (
            math.pi * jnp.bitwise_and(device, half_span - 1).astype(jnp.float32) / half_span
        )
        from_peer = jnp.stack(
            rotate(received[0], received[1], jnp.cos(offset_phase), jnp.sin(offset_phase))
        )
        from_self = jnp.stack(
            rotate(current[0], current[1], jnp.cos(offset_phase), jnp.sin(offset_phase))
        )
        current = jnp.where(is_lower, current + from_peer, received - from_self)
    unslot_cos = jnp.cos(slot_phase)[:, None, None]
    unslot_sin = -jnp.sin(slot_phase)[:, None, None]
    long_sum = jnp.sum(current[0] * unslot_cos - current[1] * unslot_sin, axis=0)
    long_part = long_sum / (2.0 * seq_total)
    output_rows = outer_conv * (long_part + skip_gain[None, :] * gated_value)
    return output_rows.astype(jnp.bfloat16)


def solution(mesh):
    placed = (
        P(("groups", "ctx"), "ch"),
        P(("groups", "ctx"), "ch"),
        P(("groups", "ctx"), "ch"),
        P(None, None, "ch"),
        P("ctx", "ch"),
        P("ch"),
    )
    return jax.shard_map(
        body, mesh=mesh, in_specs=placed, out_specs=P(("groups", "ctx"), "ch"), check_vma=False
    )
```

profile of v0, /device:TPU:0, one launch (start us, length us, event | category | flops | bytes accessed | tf_op | source)
XLA Modules:
  0.0 334.1 jit_solution(14681126279518435443)
XLA Ops:
  1.6 4.9 %collective-permute-start = (bf16[3,2,256]{1,2,0:T(8,128)(2,1)S(1)}, bf16[3,2,256]{1,2,0:T(8,128)(2,1)S(1)}, u32[]{:S(2)}, u32[]{:S(2)}) collective-permute-start(bf16[3,2,256]{1,2,0:T(8,128)(2,1)S(1)} %copy.16), channel_id=1, source_target_pairs={{0,2},{2,4},{4,6},{6,8},{8,10},{10,12},{12,14},{1,3},{3,5},{5,7},{... | collective-permute-start | bytes 9224 | tf_op jit(solution)/shard_map/ppermute | solution.py:14
  7.3 1.0 copy.20
  8.5 1.0 copy.18
  9.5 1.0 copy.19
  11.7 1.5 pad_maximum_fusion
  13.3 4.5 %collective-permute-start.1 = (f32[2,2,2,256,256]{3,4,2,1,0:T(8,128)}, f32[2,2,2,256,256]{3,4,2,1,0:T(8,128)}, u32[]{:S(2)}, u32[]{:S(2)}) collective-permute-start(f32[2,2,2,256,256]{3,4,2,1,0:T(8,128)} %pad_maximum_fusion), channel_id=1, source_target_pairs={{0,8},{2,10},{4,12},{6,14},{8,0},{10,2},{12,4},{14,6},{1,9},{3,11}... | collective-permute-start | bytes 6291464 | tf_op jit(solution)/shard_map/ppermute | solution.py:20
  17.9 89.8 %collective-permute-done.1 = f32[2,2,2,256,256]{3,4,2,1,0:T(8,128)} collective-permute-done((f32[2,2,2,256,256]{3,4,2,1,0:T(8,128)}, f32[2,2,2,256,256]{3,4,2,1,0:T(8,128)}, u32[]{:S(2)}, u32[]{:S(2)}) %collective-permute-start.1) | collective-permute-done | bytes 2097184 | tf_op jit(solution)/shard_map/ppermute | solution.py:20
  107.8 1.9 fusion.100
  109.9 3.8 %maximum_select_fusion = f32[2,2,2,256,256]{3,4,2,1,0:T(8,128)} fusion(f32[1,2,2,256,256]{3,4,2,1,0:T(8,128)S(1)} %get-tuple-element.15, f32[1,2,2,256,256]{3,4,2,1,0:T(8,128)S(1)} %get-tuple-element.14, f32[2,2,2,256,256]{3,4,2,1,0:T(8,128)} %collective-permute-done.1, pred[]{:T(512)S(6)} %eq.17, f32[1,2,2,256,256]{3,4,2,1,0:T(8,128)S(1)} %get-tuple-element.27, ...), kind=kLoop, calls=%fused_computation.1 | loop fusion | flops 2097152 | bytes 8388609 | tf_op jit(solution)/shard_map/jit(_where)/select_n | solution.py:98
  114.5 46.0 %collective-permute-done.2 = f32[2,2,2,256,256]{3,4,2,1,0:T(8,128)} collective-permute-done((f32[2,2,2,256,256]{3,4,2,1,0:T(8,128)}, f32[2,2,2,256,256]{3,4,2,1,0:T(8,128)}, u32[]{:S(2)}, u32[]{:S(2)}) %collective-permute-start.2) | collective-permute-done | bytes 2097184 | tf_op jit(solution)/shard_map/ppermute | solution.py:20
  160.5 3.1 fusion.105
  164.8 4.6 %maximum_select_fusion.1 = f32[2,2,2,256,256]{3,4,2,1,0:T(8,128)} fusion(f32[1,2,2,256,256]{3,4,2,1,0:T(8,128)S(1)} %get-tuple-element.13, f32[1,2,2,256,256]{3,4,2,1,0:T(8,128)S(1)} %get-tuple-element.12, f32[2,2,2,256,256]{3,4,2,1,0:T(8,128)} %collective-permute-done.2, pred[]{:T(512)S(6)} %eq.18, f32[1,2,2,256,256]{3,4,2,1,0:T(8,128)S(1)} %copy-done.1, ...), kind=kLoop, calls=%fused_computation.2 | loop fusion | flops 3670016 | bytes 12582914 | tf_op jit(solution)/shard_map/jit(_where)/select_n | solution.py:98
  170.1 45.5 %collective-permute-done.3 = f32[2,2,2,256,256]{3,4,2,1,0:T(8,128)S(1)} collective-permute-done((f32[2,2,2,256,256]{3,4,2,1,0:T(8,128)}, f32[2,2,2,256,256]{3,4,2,1,0:T(8,128)S(1)}, u32[]{:S(2)}, u32[]{:S(2)}) %collective-permute-start.3) | collective-permute-done | bytes 2097184 | tf_op jit(solution)/shard_map/ppermute | solution.py:20
  215.6 1.9 sub.85
  217.6 2.0 maximum_select_fusion.2
  219.6 2.0 fusion.38
  221.6 2.0 fusion.36
  223.6 2.0 fusion.1
  225.6 2.2 fusion
  228.0 1.6 fusion.12
  229.5 1.6 fusion.16
  231.1 1.6 convolution_add_fusion.1
  232.7 1.7 fusion.11
  235.2 21.9 %collective-permute-done.4 = f32[2,2,256,256]{2,3,1,0:T(8,128)S(1)} collective-permute-done((f32[2,2,256,256]{2,3,1,0:T(8,128)S(1)}, f32[2,2,256,256]{2,3,1,0:T(8,128)S(1)}, u32[]{:S(2)}, u32[]{:S(2)}) %collective-permute-start.4) | collective-permute-done | bytes 1048608 | tf_op jit(solution)/shard_map/ppermute | solution.py:20
  257.2 1.3 fusion.2
  258.5 3.3 collective-permute-start.5
  262.0 1.5 multiply_subtract_fusion.6
  263.4 19.2 %collective-permute-done.5 = f32[2,2,256,256]{2,3,1,0:T(8,128)S(1)} collective-permute-done((f32[2,2,256,256]{2,3,1,0:T(8,128)}, f32[2,2,256,256]{2,3,1,0:T(8,128)S(1)}, u32[]{:S(2)}, u32[]{:S(2)}) %collective-permute-start.5) | collective-permute-done | bytes 1048608 | tf_op jit(solution)/shard_map/ppermute | solution.py:20
  283.6 1.7 fusion.3
  285.3 4.4 %collective-permute-start.6 = (f32[2,2,256,256]{2,3,1,0:T(8,128)S(1)}, f32[2,2,256,256]{2,3,1,0:T(8,128)S(1)}, u32[]{:S(2)}, u32[]{:S(2)}) collective-permute-start(f32[2,2,256,256]{2,3,1,0:T(8,128)S(1)} %fusion.3), channel_id=1, source_target_pairs={{0,8},{2,10},{4,12},{6,14},{8,0},{10,2},{12,4},{14,6},{1,9},{3,11}... | collective-permute-start | bytes 3145736 | tf_op jit(solution)/shard_map/ppermute | solution.py:20
  289.9 1.0 copy.17
  291.2 41.0 %collective-permute-done.6 = f32[2,2,256,256]{2,3,1,0:T(8,128)S(1)} collective-permute-done((f32[2,2,256,256]{2,3,1,0:T(8,128)S(1)}, f32[2,2,256,256]{2,3,1,0:T(8,128)S(1)}, u32[]{:S(2)}, u32[]{:S(2)}) %collective-permute-start.6) | collective-permute-done | bytes 1048608 | tf_op jit(solution)/shard_map/ppermute | solution.py:20
  (60 shorter events, 11.1 us)
Async XLA Ops:
  1.6 9.0 %collective-permute-start = (bf16[3,2,256]{1,2,0:T(8,128)(2,1)S(1)}, bf16[3,2,256]{1,2,0:T(8,128)(2,1)S(1)}, u32[]{:S(2)}, u32[]{:S(2)}) collective-permute-start(bf16[3,2,256]{1,2,0:T(8,128)(2,1)S(1)} %copy.16), channel_id=1, source_target_pairs={{0,2},{2,4},{4,6},{6,8},{8,10},{10,12},{12,14},{1,3},{3,5},{5,7},{... | collective-permute-start | bytes 9224 | tf_op jit(solution)/shard_map/ppermute | solution.py:14
  13.3 94.5 %collective-permute-start.1 = (f32[2,2,2,256,256]{3,4,2,1,0:T(8,128)}, f32[2,2,2,256,256]{3,4,2,1,0:T(8,128)}, u32[]{:S(2)}, u32[]{:S(2)}) collective-permute-start(f32[2,2,2,256,256]{3,4,2,1,0:T(8,128)} %pad_maximum_fusion), channel_id=1, source_target_pairs={{0,8},{2,10},{4,12},{6,14},{8,0},{10,2},{12,4},{14,6},{1,9},{3,11}... | collective-permute-start | bytes 6291464 | tf_op jit(solution)/shard_map/ppermute | solution.py:20
  109.9 3.8 %copy-start = (f32[1,2,2,256,256]{3,4,2,1,0:T(8,128)}, f32[1,2,2,256,256]{3,4,2,1,0:T(8,128)S(1)}, u32[]{:S(2)}) copy-start(f32[1,2,2,256,256]{3,4,2,1,0:T(8,128)S(1)} %get-tuple-element.15) | copy-start | bytes 3145732
  113.6 46.9 %collective-permute-start.2 = (f32[2,2,2,256,256]{3,4,2,1,0:T(8,128)}, f32[2,2,2,256,256]{3,4,2,1,0:T(8,128)}, u32[]{:S(2)}, u32[]{:S(2)}) collective-permute-start(f32[2,2,2,256,256]{3,4,2,1,0:T(8,128)} %maximum_select_fusion), channel_id=1, source_target_pairs={{0,4},{2,6},{4,0},{6,2},{8,12},{10,14},{12,8},{14,10},{1,5},{3,7},... | collective-permute-start | bytes 6291464 | tf_op jit(solution)/shard_map/ppermute | solution.py:20
  163.6 1.2 copy-start.1
  169.4 46.2 %collective-permute-start.3 = (f32[2,2,2,256,256]{3,4,2,1,0:T(8,128)}, f32[2,2,2,256,256]{3,4,2,1,0:T(8,128)S(1)}, u32[]{:S(2)}, u32[]{:S(2)}) collective-permute-start(f32[2,2,2,256,256]{3,4,2,1,0:T(8,128)} %maximum_select_fusion.1), channel_id=1, source_target_pairs={{0,2},{2,0},{4,6},{6,4},{8,10},{10,8},{12,14},{14,12},{1,3},{3,1},... | collective-permute-start | bytes 6291464 | tf_op jit(solution)/shard_map/ppermute | solution.py:20
  234.3 22.8 %copy-start.4 = (f32[1,2,256,256]{2,3,1,0:T(8,128)}, f32[1,2,256,256]{2,3,1,0:T(8,128)S(1)}, u32[]{:S(2)}) copy-start(f32[1,2,256,256]{2,3,1,0:T(8,128)S(1)} %get-tuple-element.5) | copy-start | bytes 1572868
  234.4 22.6 %collective-permute-start.4 = (f32[2,2,256,256]{2,3,1,0:T(8,128)S(1)}, f32[2,2,256,256]{2,3,1,0:T(8,128)S(1)}, u32[]{:S(2)}, u32[]{:S(2)}) collective-permute-start(f32[2,2,256,256]{2,3,1,0:T(8,128)S(1)} %pad_maximum_fusion.1), channel_id=1, source_target_pairs={{0,2},{2,0},{4,6},{6,4},{8,10},{10,8},{12,14},{14,12},{1,3},{3,1},... | collective-permute-start | bytes 3145736 | tf_op jit(solution)/shard_map/ppermute | solution.py:20
  235.1 23.4 %copy-start.2 = (f32[1,2,256,256]{2,3,1,0:T(8,128)}, f32[1,2,256,256]{2,3,1,0:T(8,128)S(1)}, u32[]{:S(2)}) copy-start(f32[1,2,256,256]{2,3,1,0:T(8,128)S(1)} %fusion.9) | copy-start | bytes 1572868
  257.1 1.4 copy-start.6
  257.1 1.4 copy-start.8
  258.5 24.1 %collective-permute-start.5 = (f32[2,2,256,256]{2,3,1,0:T(8,128)}, f32[2,2,256,256]{2,3,1,0:T(8,128)S(1)}, u32[]{:S(2)}, u32[]{:S(2)}) collective-permute-start(f32[2,2,256,256]{2,3,1,0:T(8,128)} %fusion.2), channel_id=1, source_target_pairs={{0,4},{2,6},{4,0},{6,2},{8,12},{10,14},{12,8},{14,10},{1,5},{3,7},... | collective-permute-start | bytes 3145736 | tf_op jit(solution)/shard_map/ppermute | solution.py:20
  261.9 21.7 %copy-start.3 = (f32[1,2,256,256]{2,3,1,0:T(8,128)S(1)}, f32[1,2,256,256]{2,3,1,0:T(8,128)}, u32[]{:S(2)}) copy-start(f32[1,2,256,256]{2,3,1,0:T(8,128)} %copy-done.2) | copy-start | bytes 1572868
  262.0 21.7 %copy-start.5 = (f32[1,2,256,256]{2,3,1,0:T(8,128)S(1)}, f32[1,2,256,256]{2,3,1,0:T(8,128)}, u32[]{:S(2)}) copy-start(f32[1,2,256,256]{2,3,1,0:T(8,128)} %copy-done.4) | copy-start | bytes 1572868
  262.0 21.7 %copy-start.7 = (f32[1,2,256,256]{2,3,1,0:T(8,128)S(1)}, f32[1,2,256,256]{2,3,1,0:T(8,128)}, u32[]{:S(2)}) copy-start(f32[1,2,256,256]{2,3,1,0:T(8,128)} %copy-done.6) | copy-start | bytes 1572868
  262.0 21.7 %copy-start.9 = (f32[1,2,256,256]{2,3,1,0:T(8,128)S(1)}, f32[1,2,256,256]{2,3,1,0:T(8,128)}, u32[]{:S(2)}) copy-start(f32[1,2,256,256]{2,3,1,0:T(8,128)} %copy-done.8) | copy-start | bytes 1572868
  282.6 1.0 copy-start.10
  285.3 46.8 %collective-permute-start.6 = (f32[2,2,256,256]{2,3,1,0:T(8,128)S(1)}, f32[2,2,256,256]{2,3,1,0:T(8,128)S(1)}, u32[]{:S(2)}, u32[]{:S(2)}) collective-permute-start(f32[2,2,256,256]{2,3,1,0:T(8,128)S(1)} %fusion.3), channel_id=1, source_target_pairs={{0,8},{2,10},{4,12},{6,14},{8,0},{10,2},{12,4},{14,6},{1,9},{3,11}... | collective-permute-start | bytes 3145736 | tf_op jit(solution)/shard_map/ppermute | solution.py:20
  332.3 0.7 copy-start.11
where the time goes:
time: 335 us; the launch traced here: 334 us
  waiting for transfers between devices  263 us (79%)
  other arithmetic  27.7 us (8%)
  starting transfers between devices  19 us (6%)
  matrix products  14.5 us (4%)
  local copies, waits for them, and re-layouts  8.45 us (3%)
    ppermute x6, waiting for transfers between devices, from_partner(): return lax.ppermute(value, axis, pairs)  263 us
    ppermute x6, starting transfers between devices, from_partner(): return lax.ppermute(value, axis, pairs)  14.1 us
    select_n x3, other arithmetic, body(): current = jnp.where(is_lower, current + received, turned)  10.3 us
    sub x3, other arithmetic, body(): differ = received - current  6.82 us
  transfers between devices with their start and end apart: 7, of which 7 were waited for; matrix products, arithmetic and copies ran while one was open for 2% of the time, Pallas kernels for 0%

commit v1 on v0

v1 whole, which is shorter than its diff:
```python
import functools

import jax
import jax.numpy as jnp
import numpy as np
from jax import lax
from jax.experimental import pallas as pl
from jax.experimental.pallas import tpu as pltpu
from jax.sharding import PartitionSpec as P

LANES = 128
RIM = 8


def loop(begin, end, step, carry):
    if end - begin <= 8:
        for i in range(begin, end):
            carry = step(i, carry)
        return carry
    return lax.fori_loop(begin, end, step, carry)


def transform_table(rows):
    freq = np.arange(rows)[:, None]
    time = np.arange(rows)[None, :]
    phase = ((2 * freq + 1) * time % (4 * rows)) * (np.pi / (2 * rows))
    return np.concatenate([np.cos(phase), -np.sin(phase)], axis=0)


def split(table):
    table = np.asarray(table, np.float32)
    high = table.astype(jnp.bfloat16)
    low = (table - high.astype(np.float32)).astype(jnp.bfloat16)
    return np.stack([high, low])


def halves(value):
    high = value.astype(jnp.bfloat16)
    low = (value - high.astype(jnp.float32)).astype(jnp.bfloat16)
    return high, low


def dot(a, b):
    return jnp.dot(a, b, preferred_element_type=jnp.float32)


def lane_group(rows, width):
    return lax.broadcasted_iota(jnp.int32, (rows, LANES), 1) // width


def exchange_groups(parts, width):
    parts = list(parts)
    count = LANES // width
    group = lane_group(parts[0].shape[0], width)
    span = 1
    while span < count:
        keep = (group & span) == 0
        for q in range(count):
            if q & span == 0:
                low, high = parts[q], parts[q | span]
                parts[q] = jnp.where(keep, low, pltpu.roll(high, span * width, 1))
                parts[q | span] = jnp.where(keep, pltpu.roll(low, LANES - span * width, 1), high)
        span *= 2
    return parts


def kernel(
    devices, gate, outer, value, weight, filt, skip, table, back_table, out,
    ext, tail, rim, send_h, recv_h, send_g, recv_g, send_r, recv_r, spec, spread, prod, kept,
    rim_send, rim_recv, h_send, h_recv, g_send, g_recv, r_send, r_recv,
):
    rows, channels = gate.shape
    width = channels // devices
    count = LANES // width
    piece = rows // count
    tiles = channels // LANES
    me = lax.axis_index("ctx")

    def partner(distance):
        return lax.rem(me + distance, devices)

    barrier = pltpu.get_barrier_semaphore()

    def greet(distance, carry):
        pl.semaphore_signal(
            barrier, inc=1, device_id={"ctx": partner(distance)}, device_id_type=pl.DeviceIdType.MESH
        )
        return carry

    loop(1, devices, greet, 0)

    for i, stream in enumerate((gate, outer, value)):
        ext[i, RIM:, :] = stream[...].astype(jnp.float32)
        tail[i] = ext[i, rows:, :]

    def pack(source, send, recv):
        for tile in range(tiles):
            parts = [
                source(q * piece, tile * LANES).astype(jnp.float32) for q in range(count)
            ]
            for q, part in enumerate(exchange_groups(parts, width)):
                send[tile * count + q] = part.astype(send.dtype)
        recv[pl.ds(me, 1)] = send[pl.ds(me, 1)]

    def unpack(recv, tile):
        parts = [recv[tile * count + q].astype(jnp.float32) for q in range(count)]
        return jnp.concatenate(exchange_groups(parts, width), axis=0)

    def exchange(send, recv, send_sem, recv_sem, act):
        def step(distance, carry):
            copy = pltpu.make_async_remote_copy(
                src_ref=send.at[partner(distance)],
                dst_ref=recv.at[me],
                send_sem=send_sem.at[distance],
                recv_sem=recv_sem.at[distance],
                device_id={"ctx": partner(distance)},
                device_id_type=pl.DeviceIdType.MESH,
            )
            act(copy)
            return carry

        loop(1, devices, step, 0)

    pl.semaphore_wait(barrier, devices - 1)
    rim_copy = pltpu.make_async_remote_copy(
        src_ref=tail,
        dst_ref=rim,
        send_sem=rim_send,
        recv_sem=rim_recv,
        device_id={"ctx": partner(1)},
        device_id_type=pl.DeviceIdType.MESH,
    )
    rim_copy.start()

    pack(lambda r, c: filt[r : r + piece, c : c + LANES], send_h, recv_h)
    exchange(send_h, recv_h, h_send, h_recv, lambda copy: copy.start())

    rim_copy.wait()
    for i in range(3):
        ext[i, :RIM, :] = jnp.where(me > 0, rim[i], 0.0)

    def short(i, r, c):
        taps = weight[i].astype(jnp.float32)
        total = None
        for offset in range(taps.shape[0]):
            term = taps[offset : offset + 1, c : c + LANES] * ext[
                i, r + RIM - offset : r + RIM - offset + piece, c : c + LANES
            ]
            total = term if total is None else total + term
        return total

    def gated(r, c):
        result = short(0, r, c) * short(2, r, c)
        kept[r : r + piece, c : c + LANES] = result
        return result

    pack(gated, send_g, recv_g)
    exchange(send_g, recv_g, g_send, g_recv, lambda copy: copy.start())

    exchange(send_h, recv_h, h_send, h_recv, lambda copy: copy.wait_recv())
    for tile in range(tiles):
        taps = unpack(recv_h, tile).astype(jnp.bfloat16)
        spec[:, tile * LANES : (tile + 1) * LANES] = dot(table[0], taps) + dot(table[1], taps)
    chunk = 16
    group = lane_group(chunk, width)
    sign = 1.0 - 2.0 * (lax.broadcasted_iota(jnp.int32, (chunk, LANES), 0) % 2).astype(jnp.float32)

    def load(ref, start, tile):
        lanes = slice(tile * LANES, (tile + 1) * LANES)
        return (
            ref[pl.ds(pl.multiple_of(start, chunk), chunk), lanes],
            ref[pl.ds(pl.multiple_of(rows + start, chunk), chunk), lanes],
        )

    def shifted(blocks, tile, places):
        turned = pltpu.roll(blocks[tile], places * width, 1)
        before = pltpu.roll(blocks[tile - 1], places * width, 1) if tile > 0 else 0.0
        return jnp.where(group >= places, turned, before)

    def spread_chunk(index, carry):
        start = index * chunk
        at = pl.ds(pl.multiple_of(start, chunk), chunk)
        loaded = [load(spec, start, tile) for tile in range(tiles)]
        real = [pair[0] for pair in loaded]
        imag = [pair[1] for pair in loaded]
        for tile in range(tiles):
            both = (
                real[tile] - sign * shifted(imag, tile, 1),
                imag[tile] + sign * shifted(real, tile, 1),
            )
            for part, block in enumerate(both):

                def place(k, carry):
                    only = jnp.where(group == k, block, 0.0)
                    only = pltpu.roll(only, lax.rem(LANES - k * width, LANES), 1)
                    span = 1
                    while span < count:
                        only = only + pltpu.roll(only, span * width, 1)
                        span *= 2
                    spread[k, tile, part, at, :] = only
                    return carry

                loop(0, count, place, 0)
        return carry

    lax.fori_loop(0, rows // chunk, spread_chunk, 0)

    exchange(send_g, recv_g, g_send, g_recv, lambda copy: copy.wait_recv())
    for tile in range(tiles):
        high, low = halves(unpack(recv_g, tile))
        spec[:, tile * LANES : (tile + 1) * LANES] = (
            dot(table[0], high) + dot(table[1], high) + dot(table[0], low)
        )

    def product_chunk(index, carry):
        start = index * chunk
        at = pl.ds(pl.multiple_of(start, chunk), chunk)
        also = pl.ds(pl.multiple_of(rows + start, chunk), chunk)
        loaded = [load(spec, start, tile) for tile in range(tiles)]
        real = [pair[0] for pair in loaded]
        imag = [pair[1] for pair in loaded]

        def step(k, sums):
            sums = list(sums)
            moved_real = [shifted(real, tile, k) for tile in range(tiles)]
            moved_imag = [shifted(imag, tile, k) for tile in range(tiles)]
            for apart in range(tiles):
                kr = spread[k, apart, 0, at, :]
                ki = spread[k, apart, 1, at, :]
                for tile in range(apart, tiles):
                    xr, xi = moved_real[tile - apart], moved_imag[tile - apart]
                    sums[2 * tile] = sums[2 * tile] + (xr * kr - xi * ki)
                    sums[2 * tile + 1] = sums[2 * tile + 1] + (xr * ki + xi * kr)
            return tuple(sums)

        sums = loop(0, count, step, (jnp.zeros((chunk, LANES), jnp.float32),) * (2 * tiles))
        for tile in range(tiles):
            lanes = slice(tile * LANES, (tile + 1) * LANES)
            for where, total in ((at, sums[2 * tile]), (also, sums[2 * tile + 1])):
                high, low = halves(total)
                prod[0, where, lanes] = high
                prod[1, where, lanes] = low
        return carry

    lax.fori_loop(0, rows // chunk, product_chunk, 0)

    for tile in range(tiles):
        lanes = slice(tile * LANES, (tile + 1) * LANES)
        high, low = prod[0, :, lanes], prod[1, :, lanes]
        long_rows = dot(back_table[0], high) + dot(back_table[1], high) + dot(back_table[0], low)
        parts = [long_rows[q * piece : (q + 1) * piece] for q in range(count)]
        for q, part in enumerate(exchange_groups(parts, width)):
            send_r[tile * count + q] = part
    recv_r[pl.ds(me, 1)] = send_r[pl.ds(me, 1)]
    exchange(send_r, recv_r, r_send, r_recv, lambda copy: copy.start())

    for tile in range(tiles):
        for q in range(count):
            r, c = q * piece, tile * LANES
            ext[0, r : r + piece, c : c + LANES] = short(1, r, c)
    exchange(send_h, recv_h, h_send, h_recv, lambda copy: copy.wait_send())
    exchange(send_g, recv_g, g_send, g_recv, lambda copy: copy.wait_send())
    exchange(send_r, recv_r, r_send, r_recv, lambda copy: copy.wait_recv())
    for tile in range(tiles):
        lanes = slice(tile * LANES, (tile + 1) * LANES)
        long_part = unpack(recv_r, tile)
        out[:, lanes] = (
            ext[0, :rows, lanes] * (long_part + skip[:, lanes] * kept[:, lanes])
        ).astype(out.dtype)
    exchange(send_r, recv_r, r_send, r_recv, lambda copy: copy.wait_send())


def body(gate_stream, outer_stream, value_stream, short_weight, long_filter, skip_gain):
    devices = lax.axis_size("ctx")
    rows, channels = gate_stream.shape
    width = channels // devices
    count = LANES // width
    piece = rows // count
    tiles = channels // LANES
    table = transform_table(rows)
    filter_type = jnp.bfloat16 if piece % 16 == 0 else jnp.float32
    full = pltpu.VMEM((devices, piece, LANES), jnp.float32)
    part = pltpu.VMEM((devices, piece, LANES), filter_type)
    many = pltpu.SemaphoreType.DMA((devices,))
    vmem = pl.BlockSpec(memory_space=pltpu.VMEM)
    return pl.pallas_call(
        functools.partial(kernel, devices),
        out_shape=jax.ShapeDtypeStruct((rows, channels), jnp.bfloat16),
        in_specs=[vmem] * 8,
        out_specs=vmem,
        scratch_shapes=[
            pltpu.VMEM((3, RIM + rows, channels), jnp.float32),
            pltpu.VMEM((3, RIM, channels), jnp.float32),
            pltpu.VMEM((3, RIM, channels), jnp.float32),
            part, part, full, full, full, full,
            pltpu.VMEM((2 * rows, channels), jnp.float32),
            pltpu.VMEM((count, tiles, 2, rows, LANES), jnp.float32),
            pltpu.VMEM((2, 2 * rows, channels), jnp.bfloat16),
            pltpu.VMEM((rows, channels), jnp.float32),
            pltpu.SemaphoreType.DMA,
            pltpu.SemaphoreType.DMA,
            many, many, many, many, many, many,
        ],
        compiler_params=pltpu.CompilerParams(
            collective_id=0, has_side_effects=True, vmem_limit_bytes=48 * 1024 * 1024
        ),
        cost_estimate=pl.CostEstimate(
            flops=2 * 16 * rows * rows * channels, bytes_accessed=4 * rows * channels, transcendentals=0
        ),
    )(
        gate_stream, outer_stream, value_stream, short_weight, long_filter, skip_gain[None, :],
        jnp.asarray(split(table)), jnp.asarray(split(table.T / rows)),
    )


def solution(mesh):
    placed = (
        P(("groups", "ctx"), "ch"),
        P(("groups", "ctx"), "ch"),
        P(("groups", "ctx"), "ch"),
        P(None, None, "ch"),
        P("ctx", "ch"),
        P("ch"),
    )
    return jax.shard_map(
        body, mesh=mesh, in_specs=placed, out_specs=P(("groups", "ctx"), "ch"), check_vma=False
    )
```

time: 335 us -> 33.7 us (0.10)
  waiting for transfers between devices: 263 us -> 0 us
  other arithmetic: 27.7 us -> 0 us
  Pallas kernels: 0 us -> 25.6 us
  starting transfers between devices: 19 us -> 0 us
  matrix products: 14.5 us -> 0 us
    ppermute x7 -> x0, waiting for transfers between devices: 263 us -> none  [the longest x6 263 us: from_partner(): return lax.ppermute(value, axis, pairs)]
    pallas_call x0 -> x1, Pallas kernels: none -> 25.6 us  [body(): pl.pallas_call(functools.partial(kernel, devices), out_shape=jax.ShapeDty...]
    ppermute x7 -> x0, starting transfers between devices: 19 us -> none  [the longest x6 14.1 us: from_partner(): return lax.ppermute(value, axis, pairs)]
    dot_general x8 -> x0, matrix products: 14.5 us -> none  [the longest x2 3.75 us: along_rows(): jnp.einsum('kj,...jc->...kc', sine_part, real_part, precision=full_precis...]
    select_n x6 -> x0, other arithmetic: 13.7 us -> none  [the longest x3 10.3 us: body(): current = jnp.where(is_lower, current + received, turned)]
    sub x12 -> x0, other arithmetic: 9.5 us -> none  [the longest x3 6.82 us: body(): differ = received - current]
    unnamed x28 -> x17, local copies, waits for them, and re-layouts: 6.08 us -> 7.72 us
  transfers between devices with their start and end apart: 7 -> 0, of which waited for: 7 -> 0; matrix products, arithmetic and copies ran while one was open for 2% -> 0% of each run, Pallas kernels for 0% -> 0%
where the time goes in v1:
time: 33.7 us; the launch traced here: 33.4 us
  Pallas kernels  25.6 us (76%)
  local copies, waits for them, and re-layouts  7.72 us (23%)
    pallas_call x1, Pallas kernels, body(): pl.pallas_call(functools.partial(kernel, devices), out_shape=jax.ShapeDty...  25.6 us
    unnamed x17, local copies, waits for them, and re-layouts  7.72 us

profile of v1, /device:TPU:0, one launch (start us, length us, event | category | flops | bytes accessed | tf_op | source)
XLA Modules:
  0.0 33.4 jit_solution(7054978128569740355)
XLA Ops:
  0.0 0.0 copy-start.5
  0.0 0.7 %copy-done.5 = f32[256]{0:T(256)S(1)} copy-done((f32[256]{0:T(256)S(1)}, f32[256]{0:T(256)}, u32[]{:S(2)}) %copy-start.5) | copy-done | bytes 1048
  0.7 0.0 copy-start
  0.7 0.9 %copy-done = bf16[256,256]{1,0:T(8,128)(2,1)S(1)} copy-done((bf16[256,256]{1,0:T(8,128)(2,1)S(1)}, bf16[256,256]{1,0:T(8,128)(2,1)}, u32[]{:S(2)}) %copy-start) | copy-done | bytes 131096
  1.6 0.0 copy-start.1
  1.6 0.9 %copy-done.1 = bf16[256,256]{1,0:T(8,128)(2,1)S(1)} copy-done((bf16[256,256]{1,0:T(8,128)(2,1)S(1)}, bf16[256,256]{1,0:T(8,128)(2,1)}, u32[]{:S(2)}) %copy-start.1) | copy-done | bytes 131096
  2.5 0.0 copy-start.2
  2.5 0.9 %copy-done.2 = bf16[256,256]{1,0:T(8,128)(2,1)S(1)} copy-done((bf16[256,256]{1,0:T(8,128)(2,1)S(1)}, bf16[256,256]{1,0:T(8,128)(2,1)}, u32[]{:S(2)}) %copy-start.2) | copy-done | bytes 131096
  3.4 0.0 copy-start.3
  3.4 0.9 %copy-done.3 = bf16[256,256]{1,0:T(8,128)(2,1)S(1)} copy-done((bf16[256,256]{1,0:T(8,128)(2,1)S(1)}, bf16[256,256]{1,0:T(8,128)(2,1)}, u32[]{:S(2)}) %copy-start.3) | copy-done | bytes 131096
  4.3 0.0 copy-start.4
  4.3 0.7 %copy-done.4 = bf16[3,3,256]{2,1,0:T(4,128)(2,1)S(1)} copy-done((bf16[3,3,256]{2,1,0:T(4,128)(2,1)S(1)}, bf16[3,3,256]{2,1,0:T(4,128)(2,1)}, u32[]{:S(2)}) %copy-start.4) | copy-done | bytes 4632
  5.0 0.0 copy-start.6
  5.0 1.0 %copy-done.6 = bf16[2,256,512]{2,1,0:T(8,128)(2,1)S(1)} copy-done((bf16[2,256,512]{2,1,0:T(8,128)(2,1)S(1)}, bf16[2,256,512]{2,1,0:T(8,128)(2,1)}, u32[]{:S(2)}) %copy-start.6) | copy-done | bytes 524312
  6.0 0.0 copy-start.7
  6.0 1.0 %copy-done.7 = bf16[2,512,256]{2,1,0:T(8,128)(2,1)S(1)} copy-done((bf16[2,512,256]{2,1,0:T(8,128)(2,1)S(1)}, bf16[2,512,256]{2,1,0:T(8,128)(2,1)}, u32[]{:S(2)}) %copy-start.7) | copy-done | bytes 524312
  7.1 25.6 %shard_map.82 = bf16[256,256]{1,0:T(8,128)(2,1)S(1)} custom-call(bf16[256,256]{1,0:T(8,128)(2,1)S(1)} %copy-done, bf16[256,256]{1,0:T(8,128)(2,1)S(1)} %copy-done.1, bf16[256,256]{1,0:T(8,128)(2,1)S(1)} %copy-done.2, bf16[3,3,256]{2,1,0:T(4,128)(2,1)S(1)} %copy-done.4, bf16[256,256]{1,0:T(8,128)(2,1)S(1)} %copy-done.3, f32[1,256]{1,0:T(1,128)S(1)} %bitcast.1, ...), custom_call_target="tpu_custom_call" | custom-call | flops 536870912 | bytes 262144 | tf_op jit(solution)/shard_map/pallas_call | solution.py:286
  32.7 0.7 %copy.10 = bf16[256,256]{1,0:T(8,128)(2,1)} copy(bf16[256,256]{1,0:T(8,128)(2,1)S(1)} %shard_map.82) | data formatting | bytes 262144
Async XLA Ops:
  0.0 0.7 %copy-start.5 = (f32[256]{0:T(256)S(1)}, f32[256]{0:T(256)}, u32[]{:S(2)}) copy-start(f32[256]{0:T(256)} %param.13) | copy-start | bytes 3076
  0.7 0.9 %copy-start = (bf16[256,256]{1,0:T(8,128)(2,1)S(1)}, bf16[256,256]{1,0:T(8,128)(2,1)}, u32[]{:S(2)}) copy-start(bf16[256,256]{1,0:T(8,128)(2,1)} %gate.1) | copy-start | bytes 393220
  1.6 0.9 %copy-start.1 = (bf16[256,256]{1,0:T(8,128)(2,1)S(1)}, bf16[256,256]{1,0:T(8,128)(2,1)}, u32[]{:S(2)}) copy-start(bf16[256,256]{1,0:T(8,128)(2,1)} %outer.1) | copy-start | bytes 393220
  2.5 0.9 %copy-start.2 = (bf16[256,256]{1,0:T(8,128)(2,1)S(1)}, bf16[256,256]{1,0:T(8,128)(2,1)}, u32[]{:S(2)}) copy-start(bf16[256,256]{1,0:T(8,128)(2,1)} %value.1) | copy-start | bytes 393220
  3.4 0.9 %copy-start.3 = (bf16[256,256]{1,0:T(8,128)(2,1)S(1)}, bf16[256,256]{1,0:T(8,128)(2,1)}, u32[]{:S(2)}) copy-start(bf16[256,256]{1,0:T(8,128)(2,1)} %filt.1) | copy-start | bytes 393220
  4.3 0.7 %copy-start.4 = (bf16[3,3,256]{2,1,0:T(4,128)(2,1)S(1)}, bf16[3,3,256]{2,1,0:T(4,128)(2,1)}, u32[]{:S(2)}) copy-start(bf16[3,3,256]{2,1,0:T(4,128)(2,1)} %weight.1) | copy-start | bytes 13828
  5.0 1.0 %copy-start.6 = (bf16[2,256,512]{2,1,0:T(8,128)(2,1)S(1)}, bf16[2,256,512]{2,1,0:T(8,128)(2,1)}, u32[]{:S(2)}) copy-start(bf16[2,256,512]{2,1,0:T(8,128)(2,1)} %constant.5.clone.back_table) | copy-start | bytes 1572868
  6.0 1.0 %copy-start.7 = (bf16[2,512,256]{2,1,0:T(8,128)(2,1)S(1)}, bf16[2,512,256]{2,1,0:T(8,128)(2,1)}, u32[]{:S(2)}) copy-start(bf16[2,512,256]{2,1,0:T(8,128)(2,1)} %constant.4.clone.table) | copy-start | bytes 1572868

commit v2 on v1

v2 whole, which is shorter than its diff:
```python
import functools

import jax
import jax.numpy as jnp
import numpy as np
from jax import lax
from jax.experimental import pallas as pl
from jax.experimental.pallas import tpu as pltpu
from jax.sharding import PartitionSpec as P

LANES = 128
RIM = 8


def loop(begin, end, step, carry):
    if end - begin <= 8:
        for i in range(begin, end):
            carry = step(i, carry)
        return carry
    return lax.fori_loop(begin, end, step, carry)


def transform_table(rows):
    freq = np.arange(rows)[:, None]
    time = np.arange(rows)[None, :]
    phase = ((2 * freq + 1) * time % (4 * rows)) * (np.pi / (2 * rows))
    return np.concatenate([np.cos(phase), -np.sin(phase)], axis=0)


def split(table):
    table = np.asarray(table, np.float32)
    high = table.astype(jnp.bfloat16)
    low = (table - high.astype(np.float32)).astype(jnp.bfloat16)
    return np.stack([high, low])


def halves(value):
    high = value.astype(jnp.bfloat16)
    low = (value - high.astype(jnp.float32)).astype(jnp.bfloat16)
    return high, low


def dot(a, b):
    return jnp.dot(a, b, preferred_element_type=jnp.float32)


def lane_group(rows, width):
    return lax.broadcasted_iota(jnp.int32, (rows, LANES), 1) // width


def exchange_groups(parts, width):
    parts = list(parts)
    count = LANES // width
    group = lane_group(parts[0].shape[0], width)
    span = 1
    while span < count:
        keep = (group & span) == 0
        for q in range(count):
            if q & span == 0:
                low, high = parts[q], parts[q | span]
                parts[q] = jnp.where(keep, low, pltpu.roll(high, span * width, 1))
                parts[q | span] = jnp.where(keep, pltpu.roll(low, LANES - span * width, 1), high)
        span *= 2
    return parts


def spread_groups(block, width):
    count = LANES // width
    group = lane_group(block.shape[0], width)
    result = [block]
    span = count // 2
    while span:
        keep = (group & span) == 0
        wider = []
        for each in result:
            turned = pltpu.roll(each, span * width, 1)
            wider += [jnp.where(keep, each, turned), jnp.where(keep, turned, each)]
        result = wider
        span //= 2
    return result


def kernel(
    devices, shares, gate_hbm, outer_hbm, value_hbm, weight_hbm, filt_hbm, skip_hbm,
    table_hbm, back_hbm, out,
    gate, outer, value, weight, filt, skip, table, back_table,
    ext, tail, rim, send_h, recv_h, send_g, recv_g, send_r, recv_r, spec, spread, prod, kept,
    load_sem, rim_send, rim_recv, h_send, h_recv, g_send, g_recv, r_send, r_recv,
):
    rows, channels = gate.shape
    width = channels // (devices * shares)
    count = LANES // width
    piece = rows // count
    tiles = channels // LANES
    share_tiles = tiles // shares
    me = lax.axis_index("ctx")

    def partner(distance):
        return lax.rem(me + distance, devices)

    barrier = pltpu.get_barrier_semaphore()

    def greet(distance, carry):
        pl.semaphore_signal(
            barrier, inc=1, device_id={"ctx": partner(distance)}, device_id_type=pl.DeviceIdType.MESH
        )
        return carry

    loop(1, devices, greet, 0)

    pairs = (
        (gate_hbm, gate), (value_hbm, value), (filt_hbm, filt), (weight_hbm, weight),
        (outer_hbm, outer), (skip_hbm, skip), (table_hbm, table), (back_hbm, back_table),
    )
    loads = [pltpu.make_async_copy(src, dst, load_sem.at[i]) for i, (src, dst) in enumerate(pairs)]
    for load in loads:
        load.start()

    def place_of(tile, q):
        return divmod(tile * count + q, shares)

    def pack(source, send):
        for tile in range(tiles):
            parts = [
                source(q * piece, tile * LANES).astype(jnp.float32) for q in range(count)
            ]
            for q, part in enumerate(exchange_groups(parts, width)):
                device, share = place_of(tile, q)
                send[share, device] = part.astype(send.dtype)

    def unpack(recv, share, tile):
        parts = [recv[share, tile * count + q].astype(jnp.float32) for q in range(count)]
        return jnp.concatenate(exchange_groups(parts, width), axis=0)

    def exchange(send, recv, send_sem, recv_sem, share, act):
        def step(distance, carry):
            copy = pltpu.make_async_remote_copy(
                src_ref=send.at[share, partner(distance)],
                dst_ref=recv.at[share, me],
                send_sem=send_sem.at[share, distance],
                recv_sem=recv_sem.at[share, distance],
                device_id={"ctx": partner(distance)},
                device_id_type=pl.DeviceIdType.MESH,
            )
            act(copy)
            return carry

        loop(1, devices, step, 0)

    def keep_own(send, recv, share):
        recv[share, pl.ds(me, 1)] = send[share, pl.ds(me, 1)]

    def start(copy):
        copy.start()

    def arrived(copy):
        copy.wait_recv()

    def left(copy):
        copy.wait_send()

    loads[0].wait()
    loads[1].wait()
    loads[4].wait()
    for i, stream in enumerate((gate, outer, value)):
        ext[i, RIM:, :] = stream[...].astype(jnp.float32)
        tail[i] = ext[i, rows:, :]
    loads[2].wait()
    pack(lambda r, c: filt[r : r + piece, c : c + LANES], send_h)

    pl.semaphore_wait(barrier, devices - 1)
    rim_copy = pltpu.make_async_remote_copy(
        src_ref=tail,
        dst_ref=rim,
        send_sem=rim_send,
        recv_sem=rim_recv,
        device_id={"ctx": partner(1)},
        device_id_type=pl.DeviceIdType.MESH,
    )
    rim_copy.start()
    for share in range(shares):
        exchange(send_h, recv_h, h_send, h_recv, share, start)
        keep_own(send_h, recv_h, share)
    loads[3].wait()

    rim_copy.wait()
    for i in range(3):
        ext[i, :RIM, :] = jnp.where(me > 0, rim[i], 0.0)

    def short(i, r, c):
        taps = weight[i].astype(jnp.float32)
        total = None
        for offset in range(taps.shape[0]):
            term = taps[offset : offset + 1, c : c + LANES] * ext[
                i, r + RIM - offset : r + RIM - offset + piece, c : c + LANES
            ]
            total = term if total is None else total + term
        return total

    def gated(r, c):
        result = short(0, r, c) * short(2, r, c)
        kept[r : r + piece, c : c + LANES] = result
        return result

    pack(gated, send_g)
    for share in range(shares):
        exchange(send_g, recv_g, g_send, g_recv, share, start)
    for share in range(shares):
        keep_own(send_g, recv_g, share)
    for load in loads[5:]:
        load.wait()

    chunk = 32
    group = lane_group(chunk, width)
    sign = 1.0 - 2.0 * (lax.broadcasted_iota(jnp.int32, (chunk, LANES), 0) % 2).astype(jnp.float32)

    def read(start, tile):
        lanes = slice(tile * LANES, (tile + 1) * LANES)
        return (
            spec[pl.ds(pl.multiple_of(start, chunk), chunk), lanes],
            spec[pl.ds(pl.multiple_of(rows + start, chunk), chunk), lanes],
        )

    def shifted(blocks, tile, places):
        turned = pltpu.roll(blocks[tile], places * width, 1)
        before = pltpu.roll(blocks[tile - 1], places * width, 1) if tile > 0 else 0.0
        return jnp.where(group >= places, turned, before)

    for share in range(shares):
        exchange(send_h, recv_h, h_send, h_recv, share, arrived)
        for tile in range(share_tiles):
            taps = unpack(recv_h, share, tile).astype(jnp.bfloat16)
            spec[:, tile * LANES : (tile + 1) * LANES] = dot(table[0], taps) + dot(table[1], taps)

        def spread_chunk(index, carry):
            begin = index * chunk
            at = pl.ds(pl.multiple_of(begin, chunk), chunk)
            loaded = [read(begin, tile) for tile in range(share_tiles)]
            real = [pair[0] for pair in loaded]
            imag = [pair[1] for pair in loaded]
            for tile in range(share_tiles):
                both = (
                    real[tile] - sign * shifted(imag, tile, 1),
                    imag[tile] + sign * shifted(real, tile, 1),
                )
                for part, block in enumerate(both):
                    for k, wide in enumerate(spread_groups(block, width)):
                        spread[share, k, tile, part, at, :] = wide
            return carry

        lax.fori_loop(0, rows // chunk, spread_chunk, 0)

    for share in range(shares):
        exchange(send_g, recv_g, g_send, g_recv, share, arrived)
        for tile in range(share_tiles):
            high, low = halves(unpack(recv_g, share, tile))
            spec[:, tile * LANES : (tile + 1) * LANES] = (
                dot(table[0], high) + dot(table[1], high) + dot(table[0], low)
            )

        def product_chunk(index, carry):
            begin = index * chunk
            at = pl.ds(pl.multiple_of(begin, chunk), chunk)
            also = pl.ds(pl.multiple_of(rows + begin, chunk), chunk)
            loaded = [read(begin, tile) for tile in range(share_tiles)]
            real = [pair[0] for pair in loaded]
            imag = [pair[1] for pair in loaded]

            def step(k, sums):
                sums = list(sums)
                moved_real = [shifted(real, tile, k) for tile in range(share_tiles)]
                moved_imag = [shifted(imag, tile, k) for tile in range(share_tiles)]
                for apart in range(share_tiles):
                    kr = spread[share, k, apart, 0, at, :]
                    ki = spread[share, k, apart, 1, at, :]
                    for tile in range(apart, share_tiles):
                        xr, xi = moved_real[tile - apart], moved_imag[tile - apart]
                        sums[2 * tile] = sums[2 * tile] + (xr * kr - xi * ki)
                        sums[2 * tile + 1] = sums[2 * tile + 1] + (xr * ki + xi * kr)
                return tuple(sums)

            zero = jnp.zeros((chunk, LANES), jnp.float32)
            sums = loop(0, count, step, (zero,) * (2 * share_tiles))
            for tile in range(share_tiles):
                lanes = slice(tile * LANES, (tile + 1) * LANES)
                for where, total in ((at, sums[2 * tile]), (also, sums[2 * tile + 1])):
                    high, low = halves(total)
                    prod[0, where, lanes] = high
                    prod[1, where, lanes] = low
            return carry

        lax.fori_loop(0, rows // chunk, product_chunk, 0)

        for tile in range(share_tiles):
            lanes = slice(tile * LANES, (tile + 1) * LANES)
            high, low = prod[0, :, lanes], prod[1, :, lanes]
            long_rows = (
                dot(back_table[0], high) + dot(back_table[1], high) + dot(back_table[0], low)
            )
            parts = [long_rows[q * piece : (q + 1) * piece] for q in range(count)]
            for q, part in enumerate(exchange_groups(parts, width)):
                send_r[share, tile * count + q] = part
        exchange(send_r, recv_r, r_send, r_recv, share, start)
        keep_own(send_r, recv_r, share)

    for tile in range(tiles):
        for q in range(count):
            r, c = q * piece, tile * LANES
            at, lanes = slice(r, r + piece), slice(c, c + LANES)
            first = short(1, r, c)
            ext[0, at, lanes] = first
            kept[at, lanes] = skip[:, lanes] * kept[at, lanes] * first
    for share in range(shares):
        exchange(send_h, recv_h, h_send, h_recv, share, left)
        exchange(send_g, recv_g, g_send, g_recv, share, left)
    for share in range(shares):
        exchange(send_r, recv_r, r_send, r_recv, share, arrived)
    for tile in range(tiles):
        lanes = slice(tile * LANES, (tile + 1) * LANES)
        parts = []
        for q in range(count):
            device, share = place_of(tile, q)
            parts.append(recv_r[share, device])
        for q, part in enumerate(exchange_groups(parts, width)):
            at = slice(q * piece, (q + 1) * piece)
            out[at, lanes] = (ext[0, at, lanes] * part + kept[at, lanes]).astype(out.dtype)
    for share in range(shares):
        exchange(send_r, recv_r, r_send, r_recv, share, left)


def body(gate_stream, outer_stream, value_stream, short_weight, long_filter, skip_gain):
    devices = lax.axis_size("ctx")
    rows, channels = gate_stream.shape
    tiles = channels // LANES
    shares = 2
    while shares > 1 and (tiles % shares or rows * channels // (devices * shares * LANES) < 16):
        shares -= 1
    width = channels // (devices * shares)
    count = LANES // width
    piece = rows // count
    share_tiles = tiles // shares
    table = transform_table(rows)
    filter_type = jnp.bfloat16 if piece % 16 == 0 else jnp.float32
    full = pltpu.VMEM((shares, devices, piece, LANES), jnp.float32)
    part = pltpu.VMEM((shares, devices, piece, LANES), filter_type)
    many = pltpu.SemaphoreType.DMA((shares, devices))
    operands = (
        gate_stream, outer_stream, value_stream, short_weight, long_filter, skip_gain[None, :],
        jnp.asarray(split(table)), jnp.asarray(split(table.T / rows)),
    )
    return pl.pallas_call(
        functools.partial(kernel, devices, shares),
        out_shape=jax.ShapeDtypeStruct((rows, channels), jnp.bfloat16),
        in_specs=[pl.BlockSpec(memory_space=pltpu.HBM)] * len(operands),
        out_specs=pl.BlockSpec(memory_space=pltpu.VMEM),
        scratch_shapes=[
            *(pltpu.VMEM(each.shape, each.dtype) for each in operands),
            pltpu.VMEM((3, RIM + rows, channels), jnp.float32),
            pltpu.VMEM((3, RIM, channels), jnp.float32),
            pltpu.VMEM((3, RIM, channels), jnp.float32),
            part, part, full, full, full, full,
            pltpu.VMEM((2 * rows, share_tiles * LANES), jnp.float32),
            pltpu.VMEM((shares, count, share_tiles, 2, rows, LANES), jnp.float32),
            pltpu.VMEM((2, 2 * rows, share_tiles * LANES), jnp.bfloat16),
            pltpu.VMEM((rows, channels), jnp.float32),
            pltpu.SemaphoreType.DMA((len(operands),)),
            pltpu.SemaphoreType.DMA,
            pltpu.SemaphoreType.DMA,
            many, many, many, many, many, many,
        ],
        compiler_params=pltpu.CompilerParams(
            collective_id=0, has_side_effects=True, vmem_limit_bytes=63 * 1024 * 1024
        ),
        cost_estimate=pl.CostEstimate(
            flops=2 * 16 * rows * rows * channels, bytes_accessed=4 * rows * channels, transcendentals=0
        ),
    )(*operands)


def solution(mesh):
    placed = (
        P(("groups", "ctx"), "ch"),
        P(("groups", "ctx"), "ch"),
        P(("groups", "ctx"), "ch"),
        P(None, None, "ch"),
        P("ctx", "ch"),
        P("ch"),
    )
    return jax.shard_map(
        body, mesh=mesh, in_specs=placed, out_specs=P(("groups", "ctx"), "ch"), check_vma=False
    )
```

time: 33.7 us -> 29.7 us (0.88)
  local copies, waits for them, and re-layouts: 7.72 us -> 1.57 us
  Pallas kernels: 25.6 us -> 28 us
    unnamed x17 -> x1, local copies, waits for them, and re-layouts: 7.72 us -> 1.57 us
    pallas_call x1, Pallas kernels: 25.6 us -> 28 us  [body(): pl.pallas_call(functools.partial(kernel, devices, shares), out_shape=jax....]
where the time goes in v2:
time: 29.7 us; the launch traced here: 29.6 us
  Pallas kernels  28 us (94%)
  local copies, waits for them, and re-layouts  1.57 us (5%)
    pallas_call x1, Pallas kernels, body(): pl.pallas_call(functools.partial(kernel, devices, shares), out_shape=jax....  28 us
    unnamed x1, local copies, waits for them, and re-layouts  1.57 us

profile of v2, /device:TPU:0, one launch (start us, length us, event | category | flops | bytes accessed | tf_op | source)
XLA Modules:
  0.0 29.6 jit_solution(15934007942369942450)
XLA Ops:
  0.0 28.0 %shard_map.82 = bf16[256,256]{1,0:T(8,128)(2,1)} custom-call(bf16[256,256]{1,0:T(8,128)(2,1)} %gate_hbm.1, bf16[256,256]{1,0:T(8,128)(2,1)} %outer_hbm.1, bf16[256,256]{1,0:T(8,128)(2,1)} %value_hbm.1, bf16[3,3,256]{2,1,0:T(4,128)(2,1)} %weight_hbm.1, bf16[256,256]{1,0:T(8,128)(2,1)} %filt_hbm.1, f32[1,256]{1,0:T(1,128)} %bitcast.1, ...), custom_call_target="tpu_custom_call" | custom-call | flops 536870912 | bytes 262144 | tf_op jit(solution)/shard_map/pallas_call | solution.py:351
  28.0 1.6 %copy.10 = bf16[256,256]{1,0:T(8,128)(2,1)} copy(bf16[256,256]{1,0:T(8,128)(2,1)} %shard_map.82) | data formatting | bytes 262144

commit v3 on v2

--- a/solution.py
+++ b/solution.py
@@ -81,11 +81,11 @@
 
 
 def kernel(
-    devices, shares, gate_hbm, outer_hbm, value_hbm, weight_hbm, filt_hbm, skip_hbm,
+    devices, groups, shares, mirrored, gate_hbm, outer_hbm, value_hbm, weight_hbm, filt_hbm, skip_hbm,
     table_hbm, back_hbm, out,
     gate, outer, value, weight, filt, skip, table, back_table,
-    ext, tail, rim, send_h, recv_h, send_g, recv_g, send_r, recv_r, spec, spread, prod, kept,
-    load_sem, rim_send, rim_recv, h_send, h_recv, g_send, g_recv, r_send, r_recv,
+    ext, rim, send_h, recv_h, send_g, recv_g, send_r, recv_r, spec, spread, prod, kept, factor,
+    load_sem, rim_send, rim_recv, h_send, h_recv, m_send, m_recv, g_send, g_recv, r_send, r_recv,
 ):
     rows, channels = gate.shape
     width = channels // (devices * shares)
@@ -94,6 +94,7 @@
     tiles = channels // LANES
     share_tiles = tiles // shares
     me = lax.axis_index("ctx")
+    mine = lax.axis_index("groups")
 
     def partner(distance):
         return lax.rem(me + distance, devices)
@@ -107,30 +108,34 @@
         return carry
 
     loop(1, devices, greet, 0)
+    peers = [
+        {"groups": lax.rem(mine + distance, groups), "ctx": me}
+        for distance in range(1, groups if mirrored else 1)
+    ]
+    for peer in peers:
+        pl.semaphore_signal(barrier, inc=1, device_id=peer, device_id_type=pl.DeviceIdType.MESH)
 
     pairs = (
-        (gate_hbm, gate), (value_hbm, value), (filt_hbm, filt), (weight_hbm, weight),
+        (filt_hbm, filt), (gate_hbm, gate), (value_hbm, value), (weight_hbm, weight),
         (outer_hbm, outer), (skip_hbm, skip), (table_hbm, table), (back_hbm, back_table),
     )
     loads = [pltpu.make_async_copy(src, dst, load_sem.at[i]) for i, (src, dst) in enumerate(pairs)]
     for load in loads:
         load.start()
 
-    def place_of(tile, q):
-        return divmod(tile * count + q, shares)
-
-    def pack(source, send):
-        for tile in range(tiles):
-            parts = [
-                source(q * piece, tile * LANES).astype(jnp.float32) for q in range(count)
-            ]
+    def lanes_of(share, tile):
+        return pl.ds(pl.multiple_of((share * share_tiles + tile) * LANES, LANES), LANES)
+
+    def pack(source, send, share):
+        for tile in range(share_tiles):
+            lanes = lanes_of(share, tile)
+            parts = [source(q * piece, lanes) for q in range(count)]
             for q, part in enumerate(exchange_groups(parts, width)):
-                device, share = place_of(tile, q)
-                send[share, device] = part.astype(send.dtype)
+                send[share, tile * count + q] = part.astype(send.dtype)
 
     def unpack(recv, share, tile):
         parts = [recv[share, tile * count + q].astype(jnp.float32) for q in range(count)]
-        return jnp.concatenate(exchange_groups(parts, width), axis=0)
+        return exchange_groups(parts, width)
 
     def exchange(send, recv, send_sem, recv_sem, share, act):
         def step(distance, carry):
@@ -159,55 +164,57 @@
     def left(copy):
         copy.wait_send()
 
+    pl.semaphore_wait(barrier, devices - 1 + len(peers))
+    rim_copies = [
+        pltpu.make_async_remote_copy(
+            src_ref=stream.at[rows - rim.shape[1] :],
+            dst_ref=rim.at[i],
+            send_sem=rim_send.at[i],
+            recv_sem=rim_recv.at[i],
+            device_id={"ctx": partner(1)},
+            device_id_type=pl.DeviceIdType.MESH,
+        )
+        for i, stream in enumerate((gate_hbm, outer_hbm, value_hbm))
+    ]
+    for i in (0, 2, 1):
+        rim_copies[i].start()
+
+    order = [lax.rem(mine + i, shares) for i in range(shares)] if mirrored else range(shares)
     loads[0].wait()
-    loads[1].wait()
-    loads[4].wait()
-    for i, stream in enumerate((gate, outer, value)):
-        ext[i, RIM:, :] = stream[...].astype(jnp.float32)
-        tail[i] = ext[i, rows:, :]
-    loads[2].wait()
-    pack(lambda r, c: filt[r : r + piece, c : c + LANES], send_h)
-
-    pl.semaphore_wait(barrier, devices - 1)
-    rim_copy = pltpu.make_async_remote_copy(
-        src_ref=tail,
-        dst_ref=rim,
-        send_sem=rim_send,
-        recv_sem=rim_recv,
-        device_id={"ctx": partner(1)},
-        device_id_type=pl.DeviceIdType.MESH,
-    )
-    rim_copy.start()
-    for share in range(shares):
+    for share in order[:1] if mirrored else order:
+        pack(lambda r, lanes: filt[r : r + piece, lanes].astype(jnp.float32), send_h, share)
         exchange(send_h, recv_h, h_send, h_recv, share, start)
         keep_own(send_h, recv_h, share)
-    loads[3].wait()
-
-    rim_copy.wait()
-    for i in range(3):
-        ext[i, :RIM, :] = jnp.where(me > 0, rim[i], 0.0)
-
-    def short(i, r, c):
-        taps = weight[i].astype(jnp.float32)
+
+    def extend(i, stream):
+        ext[i, RIM:, :] = stream[...].astype(jnp.float32)
+        rim_copies[i].wait()
+        last = rim[i].astype(jnp.float32)[rim.shape[1] - RIM :]
+        ext[i, :RIM, :] = jnp.where(me > 0, last, 0.0)
+
+    def short(i, r, lanes):
+        taps = weight[i, :, lanes].astype(jnp.float32)
         total = None
         for offset in range(taps.shape[0]):
-            term = taps[offset : offset + 1, c : c + LANES] * ext[
-                i, r + RIM - offset : r + RIM - offset + piece, c : c + LANES
-            ]
+            begin = r + RIM - offset
+            term = taps[offset : offset + 1] * ext[i, begin : begin + piece, lanes]
             total = term if total is None else total + term
         return total
 
-    def gated(r, c):
-        result = short(0, r, c) * short(2, r, c)
-        kept[r : r + piece, c : c + LANES] = result
+    def gated(r, lanes):
+        result = short(0, r, lanes) * short(2, r, lanes)
+        kept[r : r + piece, lanes] = result
         return result
 
-    pack(gated, send_g)
-    for share in range(shares):
+    for load in loads[1:4]:
+        load.wait()
+    extend(0, gate)
+    extend(2, value)
+    for share in order:
+        pack(gated, send_g, share)
         exchange(send_g, recv_g, g_send, g_recv, share, start)
-    for share in range(shares):
         keep_own(send_g, recv_g, share)
-    for load in loads[5:]:
+    for load in loads[4:]:
         load.wait()
 
     chunk = 32
@@ -226,10 +233,25 @@
         before = pltpu.roll(blocks[tile - 1], places * width, 1) if tile > 0 else 0.0
         return jnp.where(group >= places, turned, before)
 
-    for share in range(shares):
-        exchange(send_h, recv_h, h_send, h_recv, share, arrived)
+    def mirror(distance, share):
+        return pltpu.make_async_remote_copy(
+            src_ref=recv_h.at[share],
+            dst_ref=recv_h.at[share],
+            send_sem=m_send.at[distance],
+            recv_sem=m_recv.at[distance],
+            device_id=peers[distance],
+            device_id_type=pl.DeviceIdType.MESH,
+        )
+
+    for turn, share in enumerate(order):
+        if turn == 0 or not mirrored:
+            exchange(send_h, recv_h, h_send, h_recv, share, arrived)
+            for distance in range(len(peers)):
+                mirror(distance, share).start()
+        else:
+            mirror(len(peers) - turn, share).wait_recv()
         for tile in range(share_tiles):
-            taps = unpack(recv_h, share, tile).astype(jnp.bfloat16)
+            taps = jnp.concatenate(unpack(recv_h, share, tile), axis=0).astype(jnp.bfloat16)
             spec[:, tile * LANES : (tile + 1) * LANES] = dot(table[0], taps) + dot(table[1], taps)
 
         def spread_chunk(index, carry):
@@ -250,10 +272,19 @@
 
         lax.fori_loop(0, rows // chunk, spread_chunk, 0)
 
-    for share in range(shares):
+    extend(1, outer)
+    for tile in range(tiles):
+        lanes = slice(tile * LANES, (tile + 1) * LANES)
+        for q in range(count):
+            at = slice(q * piece, (q + 1) * piece)
+            first = short(1, q * piece, lanes)
+            factor[at, lanes] = first
+            kept[at, lanes] = skip[:, lanes] * kept[at, lanes] * first
+
+    for share in order:
         exchange(send_g, recv_g, g_send, g_recv, share, arrived)
         for tile in range(share_tiles):
-            high, low = halves(unpack(recv_g, share, tile))
+            high, low = halves(jnp.concatenate(unpack(recv_g, share, tile), axis=0))
             spec[:, tile * LANES : (tile + 1) * LANES] = (
                 dot(table[0], high) + dot(table[1], high) + dot(table[0], low)
             )
@@ -303,33 +334,24 @@
         exchange(send_r, recv_r, r_send, r_recv, share, start)
         keep_own(send_r, recv_r, share)
 
-    for tile in range(tiles):
-        for q in range(count):
-            r, c = q * piece, tile * LANES
-            at, lanes = slice(r, r + piece), slice(c, c + LANES)
-            first = short(1, r, c)
-            ext[0, at, lanes] = first
-            kept[at, lanes] = skip[:, lanes] * kept[at, lanes] * first
-    for share in range(shares):
+    for share in order:
+        exchange(send_r, recv_r, r_send, r_recv, share, arrived)
+        for tile in range(share_tiles):
+            lanes = lanes_of(share, tile)
+            for q, part in enumerate(unpack(recv_r, share, tile)):
+                at = slice(q * piece, (q + 1) * piece)
+                out[at, lanes] = (factor[at, lanes] * part + kept[at, lanes]).astype(out.dtype)
+    for share in order[:1] if mirrored else order:
         exchange(send_h, recv_h, h_send, h_recv, share, left)
+        for distance in range(len(peers)):
+            mirror(distance, share).wait_send()
+    for share in order:
         exchange(send_g, recv_g, g_send, g_recv, share, left)
-    for share in range(shares):
-        exchange(send_r, recv_r, r_send, r_recv, share, arrived)
-    for tile in range(tiles):
-        lanes = slice(tile * LANES, (tile + 1) * LANES)
-        parts = []
-        for q in range(count):
-            device, share = place_of(tile, q)
-            parts.append(recv_r[share, device])
-        for q, part in enumerate(exchange_groups(parts, width)):
-            at = slice(q * piece, (q + 1) * piece)
-            out[at, lanes] = (ext[0, at, lanes] * part + kept[at, lanes]).astype(out.dtype)
-    for share in range(shares):
         exchange(send_r, recv_r, r_send, r_recv, share, left)
 
 
 def body(gate_stream, outer_stream, value_stream, short_weight, long_filter, skip_gain):
-    devices = lax.axis_size("ctx")
+    devices, groups = lax.axis_size("ctx"), lax.axis_size("groups")
     rows, channels = gate_stream.shape
     tiles = channels // LANES
     shares = 2
@@ -349,27 +371,30 @@
         jnp.asarray(split(table)), jnp.asarray(split(table.T / rows)),
     )
     return pl.pallas_call(
-        functools.partial(kernel, devices, shares),
+        functools.partial(kernel, devices, groups, shares, shares == groups > 1),
         out_shape=jax.ShapeDtypeStruct((rows, channels), jnp.bfloat16),
         in_specs=[pl.BlockSpec(memory_space=pltpu.HBM)] * len(operands),
         out_specs=pl.BlockSpec(memory_space=pltpu.VMEM),
         scratch_shapes=[
             *(pltpu.VMEM(each.shape, each.dtype) for each in operands),
             pltpu.VMEM((3, RIM + rows, channels), jnp.float32),
-            pltpu.VMEM((3, RIM, channels), jnp.float32),
-            pltpu.VMEM((3, RIM, channels), jnp.float32),
+            pltpu.VMEM((3, 16, channels), jnp.bfloat16),
             part, part, full, full, full, full,
             pltpu.VMEM((2 * rows, share_tiles * LANES), jnp.float32),
             pltpu.VMEM((shares, count, share_tiles, 2, rows, LANES), jnp.float32),
             pltpu.VMEM((2, 2 * rows, share_tiles * LANES), jnp.bfloat16),
             pltpu.VMEM((rows, channels), jnp.float32),
+            pltpu.VMEM((rows, channels), jnp.float32),
             pltpu.SemaphoreType.DMA((len(operands),)),
-            pltpu.SemaphoreType.DMA,
-            pltpu.SemaphoreType.DMA,
-            many, many, many, many, many, many,
+            pltpu.SemaphoreType.DMA((3,)),
+            pltpu.SemaphoreType.DMA((3,)),
+            many, many,
+            pltpu.SemaphoreType.DMA((groups,)),
+            pltpu.SemaphoreType.DMA((groups,)),
+            many, many, many, many,
         ],
         compiler_params=pltpu.CompilerParams(
-            collective_id=0, has_side_effects=True, vmem_limit_bytes=63 * 1024 * 1024
+            collective_id=0, has_side_effects=True, vmem_limit_bytes=64 * 1024 * 1024 - 320 * 1024
         ),
         cost_estimate=pl.CostEstimate(
             flops=2 * 16 * rows * rows * channels, bytes_accessed=4 * rows * channels, transcendentals=0

time: 29.7 us -> 30.8 us (1.037)
  Pallas kernels: 28 us -> 29.1 us
    pallas_call x1, Pallas kernels: 28 us -> 29.1 us  [body(): pl.pallas_call(functools.partial(kernel, devices, groups, shares, shares...]
where the time goes in v3:
time: 30.8 us; the launch traced here: 30.6 us
  Pallas kernels  29.1 us (94%)
  local copies, waits for them, and re-layouts  1.57 us (5%)
    pallas_call x1, Pallas kernels, body(): pl.pallas_call(functools.partial(kernel, devices, groups, shares, shares...  29.1 us
    unnamed x1, local copies, waits for them, and re-layouts  1.57 us

profile of v3, /device:TPU:0, one launch (start us, length us, event | category | flops | bytes accessed | tf_op | source)
XLA Modules:
  0.0 30.6 jit_solution(9471341269182005499)
XLA Ops:
  0.0 29.1 %shard_map.82 = bf16[256,256]{1,0:T(8,128)(2,1)} custom-call(bf16[256,256]{1,0:T(8,128)(2,1)} %gate_hbm.1, bf16[256,256]{1,0:T(8,128)(2,1)} %outer_hbm.1, bf16[256,256]{1,0:T(8,128)(2,1)} %value_hbm.1, bf16[3,3,256]{2,1,0:T(4,128)(2,1)} %weight_hbm.1, bf16[256,256]{1,0:T(8,128)(2,1)} %filt_hbm.1, f32[1,256]{1,0:T(1,128)} %bitcast.1, ...), custom_call_target="tpu_custom_call" | custom-call | flops 536870912 | bytes 262144 | tf_op jit(solution)/shard_map/pallas_call | solution.py:373
  29.1 1.6 %copy.10 = bf16[256,256]{1,0:T(8,128)(2,1)} copy(bf16[256,256]{1,0:T(8,128)(2,1)} %shard_map.82) | data formatting | bytes 262144

commit v4 on v3

v4 whole, which is shorter than its diff:
```python
import functools

import jax
import jax.numpy as jnp
import numpy as np
from jax import lax
from jax.experimental import pallas as pl
from jax.experimental.pallas import tpu as pltpu
from jax.sharding import PartitionSpec as P

LANES = 128
RIM = 8


def loop(begin, end, step, carry):
    if end - begin <= 8:
        for i in range(begin, end):
            carry = step(i, carry)
        return carry
    return lax.fori_loop(begin, end, step, carry)


def transform_table(rows):
    freq = np.arange(rows)[:, None]
    time = np.arange(rows)[None, :]
    phase = ((2 * freq + 1) * time % (4 * rows)) * (np.pi / (2 * rows))
    return np.concatenate([np.cos(phase), -np.sin(phase)], axis=0)


def split(table):
    table = np.asarray(table, np.float32)
    high = table.astype(jnp.bfloat16)
    low = (table - high.astype(np.float32)).astype(jnp.bfloat16)
    return np.stack([high, low])


def halves(value):
    high = value.astype(jnp.bfloat16)
    low = (value - high.astype(jnp.float32)).astype(jnp.bfloat16)
    return high, low


def dot(a, b):
    return jnp.dot(a, b, preferred_element_type=jnp.float32)


def lane_group(rows, width):
    return lax.broadcasted_iota(jnp.int32, (rows, LANES), 1) // width


def exchange_groups(parts, width):
    parts = list(parts)
    count = LANES // width
    group = lane_group(parts[0].shape[0], width)
    span = 1
    while span < count:
        keep = (group & span) == 0
        for q in range(count):
            if q & span == 0:
                low, high = parts[q], parts[q | span]
                parts[q] = jnp.where(keep, low, pltpu.roll(high, span * width, 1))
                parts[q | span] = jnp.where(keep, pltpu.roll(low, LANES - span * width, 1), high)
        span *= 2
    return parts


def spread_groups(block, width):
    count = LANES // width
    group = lane_group(block.shape[0], width)
    result = [block]
    span = count // 2
    while span:
        keep = (group & span) == 0
        wider = []
        for each in result:
            turned = pltpu.roll(each, span * width, 1)
            wider += [jnp.where(keep, each, turned), jnp.where(keep, turned, each)]
        result = wider
        span //= 2
    return result


def kernel(
    devices, shares, gate_hbm, outer_hbm, value_hbm, weight_hbm, filt_hbm, skip_hbm,
    table_hbm, back_hbm, out_hbm,
    gate, outer, value, weight, filt, skip, table, back_table,
    ext, rim, send_h, recv_h, send_g, recv_g, send_r, recv_r, spec, spec_h, spread, prod, kept, factor, out,
    load_sem, out_sem, rim_send, rim_recv, h_send, h_recv, g_send, g_recv, r_send, r_recv,
):
    rows, channels = gate.shape
    width = channels // (devices * shares)
    count = LANES // width
    piece = rows // count
    tiles = channels // LANES
    share_tiles = tiles // shares
    wide = share_tiles * LANES
    me = lax.axis_index("ctx")

    def partner(distance):
        return lax.rem(me + distance, devices)

    barrier = pltpu.get_barrier_semaphore()

    def greet(distance, carry):
        pl.semaphore_signal(
            barrier, inc=1, device_id={"ctx": partner(distance)}, device_id_type=pl.DeviceIdType.MESH
        )
        return carry

    loop(1, devices, greet, 0)
    pairs = (
        (filt_hbm, filt), (gate_hbm, gate), (value_hbm, value), (weight_hbm, weight),
        (outer_hbm, outer), (skip_hbm, skip), (table_hbm, table), (back_hbm, back_table),
    )
    loads = [pltpu.make_async_copy(src, dst, load_sem.at[i]) for i, (src, dst) in enumerate(pairs)]
    for load in loads:
        load.start()

    def lanes_of(share, tile):
        begin = (share * share_tiles + tile) * LANES
        return slice(begin, begin + LANES)

    def pack(source, share, store):
        for tile in range(share_tiles):
            lanes = lanes_of(share, tile)
            parts = [source(q * piece, piece, lanes) for q in range(count)]
            for q, part in enumerate(exchange_groups(parts, width)):
                store(share, tile * count + q, part)

    def unpack(read, tile):
        parts = [read(tile * count + q).astype(jnp.float32) for q in range(count)]
        return exchange_groups(parts, width)

    def exchange(sent, landed, send_sem, recv_sem, act):
        def step(distance, carry):
            copy = pltpu.make_async_remote_copy(
                src_ref=sent(partner(distance)),
                dst_ref=landed(me),
                send_sem=send_sem.at[distance],
                recv_sem=recv_sem.at[distance],
                device_id={"ctx": partner(distance)},
                device_id_type=pl.DeviceIdType.MESH,
            )
            act(copy)
            return carry

        loop(1, devices, step, 0)

    def filters(act):
        exchange(lambda i: send_h.at[i], lambda i: recv_h.at[i], h_send, h_recv, act)

    def values(share, act):
        exchange(
            lambda i: send_g.at[share, i], lambda i: recv_g.at[share, i],
            g_send.at[share], g_recv.at[share], act,
        )

    def results(share, act):
        exchange(
            lambda i: send_r.at[share, i], lambda i: recv_r.at[share, i],
            r_send.at[share], r_recv.at[share], act,
        )

    def start(copy):
        copy.start()

    def arrived(copy):
        copy.wait_recv()

    def left(copy):
        copy.wait_send()

    pl.semaphore_wait(barrier, devices - 1)
    rim_copies = [
        pltpu.make_async_remote_copy(
            src_ref=stream.at[rows - rim.shape[1] :],
            dst_ref=rim.at[i],
            send_sem=rim_send.at[i],
            recv_sem=rim_recv.at[i],
            device_id={"ctx": partner(1)},
            device_id_type=pl.DeviceIdType.MESH,
        )
        for i, stream in enumerate((gate_hbm, outer_hbm, value_hbm))
    ]
    for i in (0, 2, 1):
        rim_copies[i].start()

    def store_filter(share, device, part):
        send_h[device, share] = part.astype(send_h.dtype)

    def store_value(share, device, part):
        send_g[share, device] = part

    loads[0].wait()
    for share in range(shares):
        pack(lambda r, n, lanes: filt[r : r + n, lanes].astype(jnp.float32), share, store_filter)
    filters(start)

    def short(i, r, n, lanes):
        taps = weight[i, :, lanes].astype(jnp.float32)
        total = None
        for offset in range(taps.shape[0]):
            begin = r + RIM - offset
            term = taps[offset : offset + 1] * ext[i, begin : begin + n, lanes]
            total = term if total is None else total + term
        return total

    def gated(r, n, lanes):
        result = short(0, r, n, lanes) * short(2, r, n, lanes)
        kept[r : r + n, lanes] = result
        return result

    ext[:, :RIM, :] = jnp.zeros((3, RIM, channels), jnp.float32)
    for load in loads[1:4]:
        load.wait()
    ext[0, RIM:, :] = gate[...].astype(jnp.float32)
    ext[2, RIM:, :] = value[...].astype(jnp.float32)
    for share in range(shares):
        pack(gated, share, store_value)
    for i in (0, 2):
        rim_copies[i].wait()
        last = rim[i].astype(jnp.float32)[rim.shape[1] - RIM :]
        ext[i, :RIM, :] = jnp.where(me > 0, last, 0.0)
    first_lanes = lane_group(RIM, width) == 0
    for share in range(shares):
        for tile in range(share_tiles):
            block = gated(0, RIM, lanes_of(share, tile))
            for q in range(count):
                device = tile * count + q
                moved = pltpu.roll(block, (LANES - q * width) % LANES, 1)
                send_g[share, device, :RIM] = jnp.where(
                    first_lanes, moved, send_g[share, device, :RIM]
                )
        values(share, start)
    for share in range(shares):
        recv_g[share, pl.ds(me, 1)] = send_g[share, pl.ds(me, 1)]
    recv_h[pl.ds(me, 1)] = send_h[pl.ds(me, 1)]
    for load in loads[4:]:
        load.wait()

    rim_copies[1].wait()
    ext[1, :RIM, :] = jnp.where(me > 0, rim[1].astype(jnp.float32)[rim.shape[1] - RIM :], 0.0)
    ext[1, RIM:, :] = outer[...].astype(jnp.float32)
    for tile in range(tiles):
        lanes = slice(tile * LANES, (tile + 1) * LANES)
        for q in range(count):
            at = slice(q * piece, (q + 1) * piece)
            first = short(1, q * piece, piece, lanes)
            factor[at, lanes] = first
            kept[at, lanes] = skip[:, lanes] * kept[at, lanes] * first

    chunk = 32
    group = lane_group(chunk, width)
    sign = 1.0 - 2.0 * (lax.broadcasted_iota(jnp.int32, (chunk, LANES), 0) % 2).astype(jnp.float32)

    def read(ref, begin, tile):
        lanes = slice(tile * LANES, (tile + 1) * LANES)
        return (
            ref[pl.ds(pl.multiple_of(begin, chunk), chunk), lanes],
            ref[pl.ds(pl.multiple_of(rows + begin, chunk), chunk), lanes],
        )

    def shifted(blocks, tile, places):
        turned = pltpu.roll(blocks[tile], places * width, 1)
        before = pltpu.roll(blocks[tile - 1], places * width, 1) if tile > 0 else 0.0
        return jnp.where(group >= places, turned, before)

    filters(arrived)
    taps = jnp.concatenate(
        [
            jnp.concatenate(unpack(lambda i: recv_h[i, share], tile), axis=0)
            for share in range(shares)
            for tile in range(share_tiles)
        ],
        axis=1,
    ).astype(jnp.bfloat16)
    spec_h[...] = dot(table[0], taps) + dot(table[1], taps)
    for share in range(shares):

        def spread_chunk(index, carry):
            begin = index * chunk
            at = pl.ds(pl.multiple_of(begin, chunk), chunk)
            loaded = [
                read(spec_h, begin, share * share_tiles + tile) for tile in range(share_tiles)
            ]
            real = [pair[0] for pair in loaded]
            imag = [pair[1] for pair in loaded]
            for tile in range(share_tiles):
                both = (
                    real[tile] - sign * shifted(imag, tile, 1),
                    imag[tile] + sign * shifted(real, tile, 1),
                )
                for part, block in enumerate(both):
                    for k, wide in enumerate(spread_groups(block, width)):
                        spread[share, k, tile, part, at, :] = wide
            return carry

        lax.fori_loop(0, rows // chunk, spread_chunk, 0)

    for share in range(shares):
        values(share, arrived)
        block = jnp.concatenate(
            [
                jnp.concatenate(unpack(lambda i: recv_g[share, i], tile), axis=0)
                for tile in range(share_tiles)
            ],
            axis=1,
        )
        high, low = halves(block)
        both = dot(table[0], jnp.concatenate([high, low], axis=1))
        spec[...] = both[:, :wide] + both[:, wide:] + dot(table[1], high)

        def product_chunk(index, carry):
            begin = index * chunk
            at = pl.ds(pl.multiple_of(begin, chunk), chunk)
            also = pl.ds(pl.multiple_of(rows + begin, chunk), chunk)
            loaded = [read(spec, begin, tile) for tile in range(share_tiles)]
            real = [pair[0] for pair in loaded]
            imag = [pair[1] for pair in loaded]

            def step(k, sums):
                sums = list(sums)
                moved_real = [shifted(real, tile, k) for tile in range(share_tiles)]
                moved_imag = [shifted(imag, tile, k) for tile in range(share_tiles)]
                for apart in range(share_tiles):
                    kr = spread[share, k, apart, 0, at, :]
                    ki = spread[share, k, apart, 1, at, :]
                    for tile in range(apart, share_tiles):
                        xr, xi = moved_real[tile - apart], moved_imag[tile - apart]
                        sums[2 * tile] = sums[2 * tile] + (xr * kr - xi * ki)
                        sums[2 * tile + 1] = sums[2 * tile + 1] + (xr * ki + xi * kr)
                return tuple(sums)

            zero = jnp.zeros((chunk, LANES), jnp.float32)
            sums = loop(0, count, step, (zero,) * (2 * share_tiles))
            for tile in range(share_tiles):
                lanes = slice(tile * LANES, (tile + 1) * LANES)
                for where, total in ((at, sums[2 * tile]), (also, sums[2 * tile + 1])):
                    high, low = halves(total)
                    prod[where, lanes] = high
                    prod[where, slice(wide + lanes.start, wide + lanes.stop)] = low
            return carry

        lax.fori_loop(0, rows // chunk, product_chunk, 0)

        both = dot(back_table[0], prod[...])
        long_rows = both[:, :wide] + both[:, wide:] + dot(back_table[1], prod[:, :wide])
        for tile in range(share_tiles):
            lanes = slice(tile * LANES, (tile + 1) * LANES)
            parts = [long_rows[q * piece : (q + 1) * piece, lanes] for q in range(count)]
            for q, part in enumerate(exchange_groups(parts, width)):
                send_r[share, tile * count + q] = part
        results(share, start)
        recv_r[share, pl.ds(me, 1)] = send_r[share, pl.ds(me, 1)]

    leaving = []
    for share in range(shares):
        results(share, arrived)
        for tile in range(share_tiles):
            lanes = lanes_of(share, tile)
            for q, part in enumerate(unpack(lambda i: recv_r[share, i], tile)):
                at = slice(q * piece, (q + 1) * piece)
                out[at, lanes] = (factor[at, lanes] * part + kept[at, lanes]).astype(out.dtype)
        lanes = slice(share * wide, (share + 1) * wide)
        leaving.append(
            pltpu.make_async_copy(out.at[:, lanes], out_hbm.at[:, lanes], out_sem.at[share])
        )
        leaving[-1].start()
    filters(left)
    for share in range(shares):
        values(share, left)
        results(share, left)
    for copy in leaving:
        copy.wait()


def body(gate_stream, outer_stream, value_stream, short_weight, long_filter, skip_gain):
    devices = lax.axis_size("ctx")
    rows, channels = gate_stream.shape
    tiles = channels // LANES
    shares = 2
    while shares > 1 and (tiles % shares or rows * channels // (devices * shares * LANES) < 16):
        shares -= 1
    width = channels // (devices * shares)
    count = LANES // width
    piece = rows // count
    share_tiles = tiles // shares
    table = transform_table(rows)
    filter_type = jnp.bfloat16 if piece % 16 == 0 else jnp.float32
    full = pltpu.VMEM((shares, devices, piece, LANES), jnp.float32)
    part = pltpu.VMEM((devices, shares, piece, LANES), filter_type)
    many = pltpu.SemaphoreType.DMA((shares, devices))
    operands = (
        gate_stream, outer_stream, value_stream, short_weight, long_filter, skip_gain[None, :],
        jnp.asarray(split(table)), jnp.asarray(split(table.T / rows)),
    )
    return pl.pallas_call(
        functools.partial(kernel, devices, shares),
        out_shape=jax.ShapeDtypeStruct((rows, channels), jnp.bfloat16),
        in_specs=[pl.BlockSpec(memory_space=pltpu.HBM)] * len(operands),
        out_specs=pl.BlockSpec(memory_space=pltpu.HBM),
        scratch_shapes=[
            *(pltpu.VMEM(each.shape, each.dtype) for each in operands),
            pltpu.VMEM((3, RIM + rows, channels), jnp.float32),
            pltpu.VMEM((3, 16, channels), jnp.bfloat16),
            part, part, full, full, full, full,
            pltpu.VMEM((2 * rows, share_tiles * LANES), jnp.float32),
            pltpu.VMEM((2 * rows, channels), jnp.float32),
            pltpu.VMEM((shares, count, share_tiles, 2, rows, LANES), jnp.float32),
            pltpu.VMEM((2 * rows, 2 * share_tiles * LANES), jnp.bfloat16),
            pltpu.VMEM((rows, channels), jnp.float32),
            pltpu.VMEM((rows, channels), jnp.float32),
            pltpu.VMEM((rows, channels), jnp.bfloat16),
            pltpu.SemaphoreType.DMA((len(operands),)),
            pltpu.SemaphoreType.DMA((shares,)),
            pltpu.SemaphoreType.DMA((3,)),
            pltpu.SemaphoreType.DMA((3,)),
            pltpu.SemaphoreType.DMA((devices,)),
            pltpu.SemaphoreType.DMA((devices,)),
            many, many, many, many,
        ],
        compiler_params=pltpu.CompilerParams(
            collective_id=0, has_side_effects=True, vmem_limit_bytes=64 * 1024 * 1024 - 320 * 1024
        ),
        cost_estimate=pl.CostEstimate(
            flops=2 * 16 * rows * rows * channels, bytes_accessed=4 * rows * channels, transcendentals=0
        ),
    )(*operands)


def solution(mesh):
    placed = (
        P(("groups", "ctx"), "ch"),
        P(("groups", "ctx"), "ch"),
        P(("groups", "ctx"), "ch"),
        P(None, None, "ch"),
        P("ctx", "ch"),
        P("ch"),
    )
    return jax.shard_map(
        body, mesh=mesh, in_specs=placed, out_specs=P(("groups", "ctx"), "ch"), check_vma=False
    )
```

time: 30.8 us -> 29.8 us (0.968)
  Pallas kernels: 29.1 us -> 28 us
    pallas_call x1, Pallas kernels: 29.1 us -> 28 us  [body(): pl.pallas_call(functools.partial(kernel, devices, shares), out_shape=jax....]
where the time goes in v4:
time: 29.8 us; the launch traced here: 29.6 us
  Pallas kernels  28 us (94%)
  local copies, waits for them, and re-layouts  1.57 us (5%)
    pallas_call x1, Pallas kernels, body(): pl.pallas_call(functools.partial(kernel, devices, shares), out_shape=jax....  28 us
    unnamed x1, local copies, waits for them, and re-layouts  1.57 us

profile of v4, /device:TPU:0, one launch (start us, length us, event | category | flops | bytes accessed | tf_op | source)
XLA Modules:
  0.0 29.6 jit_solution(12922540906297501122)
XLA Ops:
  0.0 28.0 %shard_map.82 = bf16[256,256]{1,0:T(8,128)(2,1)} custom-call(bf16[256,256]{1,0:T(8,128)(2,1)} %gate_hbm.1, bf16[256,256]{1,0:T(8,128)(2,1)} %outer_hbm.1, bf16[256,256]{1,0:T(8,128)(2,1)} %value_hbm.1, bf16[3,3,256]{2,1,0:T(4,128)(2,1)} %weight_hbm.1, bf16[256,256]{1,0:T(8,128)(2,1)} %filt_hbm.1, f32[1,256]{1,0:T(1,128)} %bitcast.1, ...), custom_call_target="tpu_custom_call" | custom-call | flops 536870912 | bytes 262144 | tf_op jit(solution)/shard_map/pallas_call | solution.py:397
  28.1 1.6 %copy.10 = bf16[256,256]{1,0:T(8,128)(2,1)} copy(bf16[256,256]{1,0:T(8,128)(2,1)} %shard_map.82) | data formatting | bytes 262144

commit v5 on v4

--- a/solution.py
+++ b/solution.py
@@ -81,7 +81,7 @@
 
 
 def kernel(
-    devices, shares, gate_hbm, outer_hbm, value_hbm, weight_hbm, filt_hbm, skip_hbm,
+    devices, groups, shares, crossed, gate_hbm, outer_hbm, value_hbm, weight_hbm, filt_hbm, skip_hbm,
     table_hbm, back_hbm, out_hbm,
     gate, outer, value, weight, filt, skip, table, back_table,
     ext, rim, send_h, recv_h, send_g, recv_g, send_r, recv_r, spec, spec_h, spread, prod, kept, factor, out,
@@ -94,20 +94,39 @@
     tiles = channels // LANES
     share_tiles = tiles // shares
     wide = share_tiles * LANES
+    filters_held = 1 if crossed else shares
     me = lax.axis_index("ctx")
+    mine = lax.axis_index("groups")
 
     def partner(distance):
         return lax.rem(me + distance, devices)
 
+    def ahead(stage):
+        return lax.rem(mine + stage, groups) if crossed else stage
+
+    def behind(stage):
+        return lax.rem(mine + groups - stage, groups) if crossed else stage
+
+    def distances(stage):
+        return 0 if crossed and stage > 0 else 1, devices
+
+    def device_at(group, place):
+        return {"groups": group if crossed else mine, "ctx": place}
+
     barrier = pltpu.get_barrier_semaphore()
-
-    def greet(distance, carry):
-        pl.semaphore_signal(
-            barrier, inc=1, device_id={"ctx": partner(distance)}, device_id_type=pl.DeviceIdType.MESH
-        )
-        return carry
-
-    loop(1, devices, greet, 0)
+    met = 0
+    for stage in range(shares if crossed else 1):
+
+        def greet(distance, carry):
+            pl.semaphore_signal(
+                barrier, inc=1, device_id=device_at(ahead(stage), partner(distance)),
+                device_id_type=pl.DeviceIdType.MESH,
+            )
+            return carry
+
+        loop(*distances(stage), greet, 0)
+        met += devices - distances(stage)[0]
+
     pairs = (
         (filt_hbm, filt), (gate_hbm, gate), (value_hbm, value), (weight_hbm, weight),
         (outer_hbm, outer), (skip_hbm, skip), (table_hbm, table), (back_hbm, back_table),
@@ -118,47 +137,49 @@
 
     def lanes_of(share, tile):
         begin = (share * share_tiles + tile) * LANES
-        return slice(begin, begin + LANES)
+        return pl.ds(pl.multiple_of(begin, LANES), LANES)
 
     def pack(source, share, store):
         for tile in range(share_tiles):
             lanes = lanes_of(share, tile)
             parts = [source(q * piece, piece, lanes) for q in range(count)]
             for q, part in enumerate(exchange_groups(parts, width)):
-                store(share, tile * count + q, part)
+                store(tile * count + q, part)
 
     def unpack(read, tile):
         parts = [read(tile * count + q).astype(jnp.float32) for q in range(count)]
         return exchange_groups(parts, width)
 
-    def exchange(sent, landed, send_sem, recv_sem, act):
+    def exchange(span, group, sent, landed, send_sem, recv_sem, act):
         def step(distance, carry):
             copy = pltpu.make_async_remote_copy(
                 src_ref=sent(partner(distance)),
-                dst_ref=landed(me),
+                dst_ref=landed,
                 send_sem=send_sem.at[distance],
                 recv_sem=recv_sem.at[distance],
-                device_id={"ctx": partner(distance)},
+                device_id=device_at(group, partner(distance)),
                 device_id_type=pl.DeviceIdType.MESH,
             )
             act(copy)
             return carry
 
-        loop(1, devices, step, 0)
+        loop(*span, step, 0)
 
     def filters(act):
-        exchange(lambda i: send_h.at[i], lambda i: recv_h.at[i], h_send, h_recv, act)
-
-    def values(share, act):
         exchange(
-            lambda i: send_g.at[share, i], lambda i: recv_g.at[share, i],
-            g_send.at[share], g_recv.at[share], act,
-        )
-
-    def results(share, act):
+            (1, devices), mine, lambda i: send_h.at[i], recv_h.at[me], h_send, h_recv, act
+        )
+
+    def values(stage, act):
         exchange(
-            lambda i: send_r.at[share, i], lambda i: recv_r.at[share, i],
-            r_send.at[share], r_recv.at[share], act,
+            distances(stage), ahead(stage), lambda i: send_g.at[ahead(stage), i],
+            recv_g.at[mine if crossed else stage, me], g_send.at[stage], g_recv.at[stage], act,
+        )
+
+    def results(stage, act):
+        exchange(
+            distances(stage), behind(stage), lambda i: send_r.at[behind(stage), i],
+            recv_r.at[mine if crossed else stage, me], r_send.at[stage], r_recv.at[stage], act,
         )
 
     def start(copy):
@@ -170,14 +191,14 @@
     def left(copy):
         copy.wait_send()
 
-    pl.semaphore_wait(barrier, devices - 1)
+    pl.semaphore_wait(barrier, met)
     rim_copies = [
         pltpu.make_async_remote_copy(
             src_ref=stream.at[rows - rim.shape[1] :],
             dst_ref=rim.at[i],
             send_sem=rim_send.at[i],
             recv_sem=rim_recv.at[i],
-            device_id={"ctx": partner(1)},
+            device_id={"groups": mine, "ctx": partner(1)},
             device_id_type=pl.DeviceIdType.MESH,
         )
         for i, stream in enumerate((gate_hbm, outer_hbm, value_hbm))
@@ -185,15 +206,16 @@
     for i in (0, 2, 1):
         rim_copies[i].start()
 
-    def store_filter(share, device, part):
-        send_h[device, share] = part.astype(send_h.dtype)
-
-    def store_value(share, device, part):
-        send_g[share, device] = part
-
     loads[0].wait()
-    for share in range(shares):
-        pack(lambda r, n, lanes: filt[r : r + n, lanes].astype(jnp.float32), share, store_filter)
+    for held in range(filters_held):
+
+        def store_filter(device, part):
+            send_h[device, held] = part.astype(send_h.dtype)
+
+        pack(
+            lambda r, n, lanes: filt[r : r + n, lanes].astype(jnp.float32),
+            mine if crossed else held, store_filter,
+        )
     filters(start)
 
     def short(i, r, n, lanes):
@@ -215,14 +237,19 @@
         load.wait()
     ext[0, RIM:, :] = gate[...].astype(jnp.float32)
     ext[2, RIM:, :] = value[...].astype(jnp.float32)
-    for share in range(shares):
-        pack(gated, share, store_value)
+    for stage in range(shares):
+
+        def store_value(device, part):
+            send_g[ahead(stage), device] = part
+
+        pack(gated, ahead(stage), store_value)
     for i in (0, 2):
         rim_copies[i].wait()
         last = rim[i].astype(jnp.float32)[rim.shape[1] - RIM :]
         ext[i, :RIM, :] = jnp.where(me > 0, last, 0.0)
     first_lanes = lane_group(RIM, width) == 0
-    for share in range(shares):
+    for stage in range(shares):
+        share = ahead(stage)
         for tile in range(share_tiles):
             block = gated(0, RIM, lanes_of(share, tile))
             for q in range(count):
@@ -231,9 +258,9 @@
                 send_g[share, device, :RIM] = jnp.where(
                     first_lanes, moved, send_g[share, device, :RIM]
                 )
-        values(share, start)
-    for share in range(shares):
-        recv_g[share, pl.ds(me, 1)] = send_g[share, pl.ds(me, 1)]
+        values(stage, start)
+    for stage in range(1 if crossed else shares):
+        recv_g[behind(stage), pl.ds(me, 1)] = send_g[ahead(stage), pl.ds(me, 1)]
     recv_h[pl.ds(me, 1)] = send_h[pl.ds(me, 1)]
     for load in loads[4:]:
         load.wait()
@@ -268,20 +295,20 @@
     filters(arrived)
     taps = jnp.concatenate(
         [
-            jnp.concatenate(unpack(lambda i: recv_h[i, share], tile), axis=0)
-            for share in range(shares)
+            jnp.concatenate(unpack(lambda i: recv_h[i, held], tile), axis=0)
+            for held in range(filters_held)
             for tile in range(share_tiles)
         ],
         axis=1,
     ).astype(jnp.bfloat16)
     spec_h[...] = dot(table[0], taps) + dot(table[1], taps)
-    for share in range(shares):
+    for held in range(filters_held):
 
         def spread_chunk(index, carry):
             begin = index * chunk
             at = pl.ds(pl.multiple_of(begin, chunk), chunk)
             loaded = [
-                read(spec_h, begin, share * share_tiles + tile) for tile in range(share_tiles)
+                read(spec_h, begin, held * share_tiles + tile) for tile in range(share_tiles)
             ]
             real = [pair[0] for pair in loaded]
             imag = [pair[1] for pair in loaded]
@@ -292,13 +319,14 @@
                 )
                 for part, block in enumerate(both):
                     for k, wide in enumerate(spread_groups(block, width)):
-                        spread[share, k, tile, part, at, :] = wide
+                        spread[held, k, tile, part, at, :] = wide
             return carry
 
         lax.fori_loop(0, rows // chunk, spread_chunk, 0)
 
-    for share in range(shares):
-        values(share, arrived)
+    for stage in range(shares):
+        share, held = behind(stage), 0 if crossed else stage
+        values(stage, arrived)
         block = jnp.concatenate(
             [
                 jnp.concatenate(unpack(lambda i: recv_g[share, i], tile), axis=0)
@@ -323,8 +351,8 @@
                 moved_real = [shifted(real, tile, k) for tile in range(share_tiles)]
                 moved_imag = [shifted(imag, tile, k) for tile in range(share_tiles)]
                 for apart in range(share_tiles):
-                    kr = spread[share, k, apart, 0, at, :]
-                    ki = spread[share, k, apart, 1, at, :]
+                    kr = spread[held, k, apart, 0, at, :]
+                    ki = spread[held, k, apart, 1, at, :]
                     for tile in range(apart, share_tiles):
                         xr, xi = moved_real[tile - apart], moved_imag[tile - apart]
                         sums[2 * tile] = sums[2 * tile] + (xr * kr - xi * ki)
@@ -350,37 +378,41 @@
             parts = [long_rows[q * piece : (q + 1) * piece, lanes] for q in range(count)]
             for q, part in enumerate(exchange_groups(parts, width)):
                 send_r[share, tile * count + q] = part
-        results(share, start)
-        recv_r[share, pl.ds(me, 1)] = send_r[share, pl.ds(me, 1)]
+        results(stage, start)
+        if stage == 0 or not crossed:
+            recv_r[share, pl.ds(me, 1)] = send_r[share, pl.ds(me, 1)]
 
     leaving = []
-    for share in range(shares):
-        results(share, arrived)
+    for stage in range(shares):
+        share = ahead(stage)
+        results(stage, arrived)
         for tile in range(share_tiles):
             lanes = lanes_of(share, tile)
             for q, part in enumerate(unpack(lambda i: recv_r[share, i], tile)):
                 at = slice(q * piece, (q + 1) * piece)
                 out[at, lanes] = (factor[at, lanes] * part + kept[at, lanes]).astype(out.dtype)
-        lanes = slice(share * wide, (share + 1) * wide)
+        lanes = pl.ds(pl.multiple_of(share * wide, LANES), wide)
         leaving.append(
-            pltpu.make_async_copy(out.at[:, lanes], out_hbm.at[:, lanes], out_sem.at[share])
+            pltpu.make_async_copy(out.at[:, lanes], out_hbm.at[:, lanes], out_sem.at[stage])
         )
         leaving[-1].start()
     filters(left)
-    for share in range(shares):
-        values(share, left)
-        results(share, left)
+    for stage in range(shares):
+        values(stage, left)
+        results(stage, left)
     for copy in leaving:
         copy.wait()
 
 
 def body(gate_stream, outer_stream, value_stream, short_weight, long_filter, skip_gain):
-    devices = lax.axis_size("ctx")
+    devices, groups = lax.axis_size("ctx"), lax.axis_size("groups")
     rows, channels = gate_stream.shape
     tiles = channels // LANES
     shares = 2
     while shares > 1 and (tiles % shares or rows * channels // (devices * shares * LANES) < 16):
         shares -= 1
+    crossed = shares == groups > 1
+    held = 1 if crossed else shares
     width = channels // (devices * shares)
     count = LANES // width
     piece = rows // count
@@ -388,14 +420,14 @@
     table = transform_table(rows)
     filter_type = jnp.bfloat16 if piece % 16 == 0 else jnp.float32
     full = pltpu.VMEM((shares, devices, piece, LANES), jnp.float32)
-    part = pltpu.VMEM((devices, shares, piece, LANES), filter_type)
+    part = pltpu.VMEM((devices, held, piece, LANES), filter_type)
     many = pltpu.SemaphoreType.DMA((shares, devices))
     operands = (
         gate_stream, outer_stream, value_stream, short_weight, long_filter, skip_gain[None, :],
         jnp.asarray(split(table)), jnp.asarray(split(table.T / rows)),
     )
     return pl.pallas_call(
-        functools.partial(kernel, devices, shares),
+        functools.partial(kernel, devices, groups, shares, crossed),
         out_shape=jax.ShapeDtypeStruct((rows, channels), jnp.bfloat16),
         in_specs=[pl.BlockSpec(memory_space=pltpu.HBM)] * len(operands),
         out_specs=pl.BlockSpec(memory_space=pltpu.HBM),
@@ -405,8 +437,8 @@
             pltpu.VMEM((3, 16, channels), jnp.bfloat16),
             part, part, full, full, full, full,
             pltpu.VMEM((2 * rows, share_tiles * LANES), jnp.float32),
-            pltpu.VMEM((2 * rows, channels), jnp.float32),
-            pltpu.VMEM((shares, count, share_tiles, 2, rows, LANES), jnp.float32),
+            pltpu.VMEM((2 * rows, held * share_tiles * LANES), jnp.float32),
+            pltpu.VMEM((held, count, share_tiles, 2, rows, LANES), jnp.float32),
             pltpu.VMEM((2 * rows, 2 * share_tiles * LANES), jnp.bfloat16),
             pltpu.VMEM((rows, channels), jnp.float32),
             pltpu.VMEM((rows, channels), jnp.float32),

time: 29.8 us -> 28.5 us (0.956)
  Pallas kernels: 28 us -> 26.8 us
    pallas_call x1, Pallas kernels: 28 us -> 26.8 us  [body(): pl.pallas_call(functools.partial(kernel, devices, groups, shares, crossed...]
where the time goes in v5:
time: 28.5 us; the launch traced here: 28.4 us
  Pallas kernels  26.8 us (94%)
  local copies, waits for them, and re-layouts  1.57 us (6%)
    pallas_call x1, Pallas kernels, body(): pl.pallas_call(functools.partial(kernel, devices, groups, shares, crossed...  26.8 us
    unnamed x1, local copies, waits for them, and re-layouts  1.57 us

profile of v5, /device:TPU:0, one launch (start us, length us, event | category | flops | bytes accessed | tf_op | source)
XLA Modules:
  0.0 28.4 jit_solution(6907506828516394866)
XLA Ops:
  0.0 26.8 %shard_map.82 = bf16[256,256]{1,0:T(8,128)(2,1)} custom-call(bf16[256,256]{1,0:T(8,128)(2,1)} %gate_hbm.1, bf16[256,256]{1,0:T(8,128)(2,1)} %outer_hbm.1, bf16[256,256]{1,0:T(8,128)(2,1)} %value_hbm.1, bf16[3,3,256]{2,1,0:T(4,128)(2,1)} %weight_hbm.1, bf16[256,256]{1,0:T(8,128)(2,1)} %filt_hbm.1, f32[1,256]{1,0:T(1,128)} %bitcast.1, ...), custom_call_target="tpu_custom_call" | custom-call | flops 536870912 | bytes 262144 | tf_op jit(solution)/shard_map/pallas_call | solution.py:429
  26.8 1.6 %copy.10 = bf16[256,256]{1,0:T(8,128)(2,1)} copy(bf16[256,256]{1,0:T(8,128)(2,1)} %shard_map.82) | data formatting | bytes 262144

commit v6 on v5

--- a/solution.py
+++ b/solution.py
@@ -258,7 +258,8 @@
                 send_g[share, device, :RIM] = jnp.where(
                     first_lanes, moved, send_g[share, device, :RIM]
                 )
-        values(stage, start)
+        if stage == 0:
+            values(stage, start)
     for stage in range(1 if crossed else shares):
         recv_g[behind(stage), pl.ds(me, 1)] = send_g[ahead(stage), pl.ds(me, 1)]
     recv_h[pl.ds(me, 1)] = send_h[pl.ds(me, 1)]
@@ -291,6 +292,10 @@
         turned = pltpu.roll(blocks[tile], places * width, 1)
         before = pltpu.roll(blocks[tile - 1], places * width, 1) if tile > 0 else 0.0
         return jnp.where(group >= places, turned, before)
+
+    for stage in range(1, shares):
+        values(stage - 1, left)
+        values(stage, start)
 
     filters(arrived)
     taps = jnp.concatenate(
@@ -397,8 +402,8 @@
         )
         leaving[-1].start()
     filters(left)
+    values(shares - 1, left)
     for stage in range(shares):
-        values(stage, left)
         results(stage, left)
     for copy in leaving:
         copy.wait()

time: 28.5 us -> 28.7 us (level)
  no operation moved by 1% of the time
where the time goes in v6:
time: 28.7 us; the launch traced here: 28.6 us
  Pallas kernels  27 us (94%)
  local copies, waits for them, and re-layouts  1.57 us (5%)
    pallas_call x1, Pallas kernels, body(): pl.pallas_call(functools.partial(kernel, devices, groups, shares, crossed...  27 us
    unnamed x1, local copies, waits for them, and re-layouts  1.57 us

profile of v6, /device:TPU:0, one launch (start us, length us, event | category | flops | bytes accessed | tf_op | source)
XLA Modules:
  0.0 28.6 jit_solution(11673283531437406566)
XLA Ops:
  0.0 27.0 %shard_map.82 = bf16[256,256]{1,0:T(8,128)(2,1)} custom-call(bf16[256,256]{1,0:T(8,128)(2,1)} %gate_hbm.1, bf16[256,256]{1,0:T(8,128)(2,1)} %outer_hbm.1, bf16[256,256]{1,0:T(8,128)(2,1)} %value_hbm.1, bf16[3,3,256]{2,1,0:T(4,128)(2,1)} %weight_hbm.1, bf16[256,256]{1,0:T(8,128)(2,1)} %filt_hbm.1, f32[1,256]{1,0:T(1,128)} %bitcast.1, ...), custom_call_target="tpu_custom_call" | custom-call | flops 536870912 | bytes 262144 | tf_op jit(solution)/shard_map/pallas_call | solution.py:434
  27.0 1.6 %copy.10 = bf16[256,256]{1,0:T(8,128)(2,1)} copy(bf16[256,256]{1,0:T(8,128)(2,1)} %shard_map.82) | data formatting | bytes 262144

commit v7 on v5

--- a/solution.py
+++ b/solution.py
@@ -280,11 +280,16 @@
     group = lane_group(chunk, width)
     sign = 1.0 - 2.0 * (lax.broadcasted_iota(jnp.int32, (chunk, LANES), 0) % 2).astype(jnp.float32)
 
+    def rows_at(begin):
+        if isinstance(begin, int):
+            return slice(begin, begin + chunk)
+        return pl.ds(pl.multiple_of(begin, chunk), chunk)
+
     def read(ref, begin, tile):
         lanes = slice(tile * LANES, (tile + 1) * LANES)
         return (
-            ref[pl.ds(pl.multiple_of(begin, chunk), chunk), lanes],
-            ref[pl.ds(pl.multiple_of(rows + begin, chunk), chunk), lanes],
+            ref[rows_at(begin), lanes],
+            ref[rows_at(rows + begin), lanes],
         )
 
     def shifted(blocks, tile, places):
@@ -306,7 +311,7 @@
 
         def spread_chunk(index, carry):
             begin = index * chunk
-            at = pl.ds(pl.multiple_of(begin, chunk), chunk)
+            at = rows_at(begin)
             loaded = [
                 read(spec_h, begin, held * share_tiles + tile) for tile in range(share_tiles)
             ]
@@ -322,7 +327,7 @@
                         spread[held, k, tile, part, at, :] = wide
             return carry
 
-        lax.fori_loop(0, rows // chunk, spread_chunk, 0)
+        loop(0, rows // chunk, spread_chunk, 0)
 
     for stage in range(shares):
         share, held = behind(stage), 0 if crossed else stage
@@ -340,8 +345,8 @@
 
         def product_chunk(index, carry):
             begin = index * chunk
-            at = pl.ds(pl.multiple_of(begin, chunk), chunk)
-            also = pl.ds(pl.multiple_of(rows + begin, chunk), chunk)
+            at = rows_at(begin)
+            also = rows_at(rows + begin)
             loaded = [read(spec, begin, tile) for tile in range(share_tiles)]
             real = [pair[0] for pair in loaded]
             imag = [pair[1] for pair in loaded]
@@ -369,7 +374,7 @@
                     prod[where, slice(wide + lanes.start, wide + lanes.stop)] = low
             return carry
 
-        lax.fori_loop(0, rows // chunk, product_chunk, 0)
+        loop(0, rows // chunk, product_chunk, 0)
 
         both = dot(back_table[0], prod[...])
         long_rows = both[:, :wide] + both[:, wide:] + dot(back_table[1], prod[:, :wide])

time: 28.5 us -> 28.6 us (level)
  no operation moved by 1% of the time
where the time goes in v7:
time: 28.6 us; the launch traced here: 28.5 us
  Pallas kernels  26.9 us (94%)
  local copies, waits for them, and re-layouts  1.57 us (5%)
    pallas_call x1, Pallas kernels, body(): pl.pallas_call(functools.partial(kernel, devices, groups, shares, crossed...  26.9 us
    unnamed x1, local copies, waits for them, and re-layouts  1.57 us

profile of v7, /device:TPU:0, one launch (start us, length us, event | category | flops | bytes accessed | tf_op | source)
XLA Modules:
  0.0 28.5 jit_solution(10492094766024980091)
XLA Ops:
  0.0 26.9 %shard_map.82 = bf16[256,256]{1,0:T(8,128)(2,1)} custom-call(bf16[256,256]{1,0:T(8,128)(2,1)} %gate_hbm.1, bf16[256,256]{1,0:T(8,128)(2,1)} %outer_hbm.1, bf16[256,256]{1,0:T(8,128)(2,1)} %value_hbm.1, bf16[3,3,256]{2,1,0:T(4,128)(2,1)} %weight_hbm.1, bf16[256,256]{1,0:T(8,128)(2,1)} %filt_hbm.1, f32[1,256]{1,0:T(1,128)} %bitcast.1, ...), custom_call_target="tpu_custom_call" | custom-call | flops 536870912 | bytes 262144 | tf_op jit(solution)/shard_map/pallas_call | solution.py:434
  26.9 1.6 %copy.10 = bf16[256,256]{1,0:T(8,128)(2,1)} copy(bf16[256,256]{1,0:T(8,128)(2,1)} %shard_map.82) | data formatting | bytes 262144

commit v8 on v7

--- a/solution.py
+++ b/solution.py
@@ -82,10 +82,10 @@
 
 def kernel(
     devices, groups, shares, crossed, gate_hbm, outer_hbm, value_hbm, weight_hbm, filt_hbm, skip_hbm,
-    table_hbm, back_hbm, out_hbm,
+    table_hbm, back_hbm, out,
     gate, outer, value, weight, filt, skip, table, back_table,
-    ext, rim, send_h, recv_h, send_g, recv_g, send_r, recv_r, spec, spec_h, spread, prod, kept, factor, out,
-    load_sem, out_sem, rim_send, rim_recv, h_send, h_recv, g_send, g_recv, r_send, r_recv,
+    ext, rim, send_h, recv_h, send_g, recv_g, send_r, recv_r, spec, spec_h, spread, prod, kept, factor,
+    load_sem, rim_send, rim_recv, h_send, h_recv, g_send, g_recv, r_send, r_recv,
 ):
     rows, channels = gate.shape
     width = channels // (devices * shares)
@@ -387,7 +387,6 @@
         if stage == 0 or not crossed:
             recv_r[share, pl.ds(me, 1)] = send_r[share, pl.ds(me, 1)]
 
-    leaving = []
     for stage in range(shares):
         share = ahead(stage)
         results(stage, arrived)
@@ -396,17 +395,10 @@
             for q, part in enumerate(unpack(lambda i: recv_r[share, i], tile)):
                 at = slice(q * piece, (q + 1) * piece)
                 out[at, lanes] = (factor[at, lanes] * part + kept[at, lanes]).astype(out.dtype)
-        lanes = pl.ds(pl.multiple_of(share * wide, LANES), wide)
-        leaving.append(
-            pltpu.make_async_copy(out.at[:, lanes], out_hbm.at[:, lanes], out_sem.at[stage])
-        )
-        leaving[-1].start()
     filters(left)
     for stage in range(shares):
         values(stage, left)
         results(stage, left)
-    for copy in leaving:
-        copy.wait()
 
 
 def body(gate_stream, outer_stream, value_stream, short_weight, long_filter, skip_gain):
@@ -435,7 +427,7 @@
         functools.partial(kernel, devices, groups, shares, crossed),
         out_shape=jax.ShapeDtypeStruct((rows, channels), jnp.bfloat16),
         in_specs=[pl.BlockSpec(memory_space=pltpu.HBM)] * len(operands),
-        out_specs=pl.BlockSpec(memory_space=pltpu.HBM),
+        out_specs=pl.BlockSpec(memory_space=pltpu.VMEM),
         scratch_shapes=[
             *(pltpu.VMEM(each.shape, each.dtype) for each in operands),
             pltpu.VMEM((3, RIM + rows, channels), jnp.float32),
@@ -447,9 +439,7 @@
             pltpu.VMEM((2 * rows, 2 * share_tiles * LANES), jnp.bfloat16),
             pltpu.VMEM((rows, channels), jnp.float32),
             pltpu.VMEM((rows, channels), jnp.float32),
-            pltpu.VMEM((rows, channels), jnp.bfloat16),
             pltpu.SemaphoreType.DMA((len(operands),)),
-            pltpu.SemaphoreType.DMA((shares,)),
             pltpu.SemaphoreType.DMA((3,)),
             pltpu.SemaphoreType.DMA((3,)),
             pltpu.SemaphoreType.DMA((devices,)),
@@ -457,7 +447,7 @@
             many, many, many, many,
         ],
         compiler_params=pltpu.CompilerParams(
-            collective_id=0, has_side_effects=True, vmem_limit_bytes=64 * 1024 * 1024 - 320 * 1024
+            collective_id=0, has_side_effects=True, vmem_limit_bytes=55040 * 1024
         ),
         cost_estimate=pl.CostEstimate(
             flops=2 * 16 * rows * rows * channels, bytes_accessed=4 * rows * channels, transcendentals=0

time: 28.6 us -> 28.6 us (level)
  Pallas kernels: 26.9 us -> 26.3 us
  local copies, waits for them, and re-layouts: 1.57 us -> 2.03 us
    pallas_call x1, Pallas kernels: 26.9 us -> 26.3 us  [body(): pl.pallas_call(functools.partial(kernel, devices, groups, shares, crossed...]
    unnamed x1 -> x5, local copies, waits for them, and re-layouts: 1.57 us -> 2.03 us
where the time goes in v8:
time: 28.6 us; the launch traced here: 28.3 us
  Pallas kernels  26.3 us (92%)
  local copies, waits for them, and re-layouts  2.03 us (7%)
    pallas_call x1, Pallas kernels, body(): pl.pallas_call(functools.partial(kernel, devices, groups, shares, crossed...  26.3 us
    unnamed x5, local copies, waits for them, and re-layouts  2.03 us

profile of v8, /device:TPU:0, one launch (start us, length us, event | category | flops | bytes accessed | tf_op | source)
XLA Modules:
  0.0 28.3 jit_solution(3513754791609947656)
XLA Ops:
  0.0 0.0 copy-start.1
  0.0 0.7 %copy-done.1 = f32[256]{0:T(256)S(1)} copy-done((f32[256]{0:T(256)S(1)}, f32[256]{0:T(256)}, u32[]{:S(2)}) %copy-start.1) | copy-done | bytes 1048
  0.7 0.0 copy-start
  0.7 0.7 %copy-done = bf16[3,3,256]{2,1,0:T(4,128)(2,1)S(1)} copy-done((bf16[3,3,256]{2,1,0:T(4,128)(2,1)S(1)}, bf16[3,3,256]{2,1,0:T(4,128)(2,1)}, u32[]{:S(2)}) %copy-start) | copy-done | bytes 4632
  1.4 26.3 %shard_map.82 = bf16[256,256]{1,0:T(8,128)(2,1)S(1)} custom-call(bf16[256,256]{1,0:T(8,128)(2,1)} %gate_hbm.1, bf16[256,256]{1,0:T(8,128)(2,1)} %outer_hbm.1, bf16[256,256]{1,0:T(8,128)(2,1)} %value_hbm.1, bf16[3,3,256]{2,1,0:T(4,128)(2,1)S(1)} %copy-done, bf16[256,256]{1,0:T(8,128)(2,1)} %filt_hbm.1, f32[1,256]{1,0:T(1,128)S(1)} %bitcast.1, ...), custom_call_target="tpu_custom_call" | custom-call | flops 536870912 | bytes 262144 | tf_op jit(solution)/shard_map/pallas_call | solution.py:426
  27.7 0.7 %copy.10 = bf16[256,256]{1,0:T(8,128)(2,1)} copy(bf16[256,256]{1,0:T(8,128)(2,1)S(1)} %shard_map.82) | data formatting | bytes 262144
Async XLA Ops:
  0.0 0.7 %copy-start.1 = (f32[256]{0:T(256)S(1)}, f32[256]{0:T(256)}, u32[]{:S(2)}) copy-start(f32[256]{0:T(256)} %param.13) | copy-start | bytes 3076
  0.7 0.7 %copy-start = (bf16[3,3,256]{2,1,0:T(4,128)(2,1)S(1)}, bf16[3,3,256]{2,1,0:T(4,128)(2,1)}, u32[]{:S(2)}) copy-start(bf16[3,3,256]{2,1,0:T(4,128)(2,1)} %weight_hbm.1) | copy-start | bytes 13828
